TPU v7x, 128 devices: a whole 4x4x4 slice. The times are simulated.
128 devices in a mesh: depth: 4 (over y), row: 8 (over x_lo, z), col: 4 (over x_hi, core).
Axes of the slice: x: 4 (x_hi: 2, x_lo: 2; x = x_hi * 2 + x_lo), y: 4, z: 4, core: 2. Of those that a mesh axis runs over, the one named last changes fastest.
Arguments:
- tokens: bfloat16 [768, 8192], P(('row', 'col'), 'depth'), may hold values from -6 to 6
- cotangent: bfloat16 [768, 8192], P(('row', 'col'), 'depth'), may hold values from -6 to 6
- gate_weight: bfloat16 [8192, 28672], P('depth', ('row', 'col')), may hold values from -0.0625 to 0.0625
- up_weight: bfloat16 [8192, 28672], P('depth', ('row', 'col')), may hold values from -0.0625 to 0.0625
- down_weight: bfloat16 [28672, 8192], P(('row', 'col'), 'depth'), may hold values from -0.03125 to 0.03125
Outputs:
- tokens_grad: bfloat16 [768, 8192], P(('row', 'col'), 'depth')
- gate_grad: bfloat16 [8192, 28672], P('depth', ('row', 'col'))
- up_grad: bfloat16 [8192, 28672], P('depth', ('row', 'col'))
- down_grad: bfloat16 [28672, 8192], P(('row', 'col'), 'depth')
All inputs are finite; a program needn't handle non-finite values.
Results may differ from a plain program's by a relative error of at most 0.005.
Values may be sent and summed in bfloat16 or wider, within the bound.
No kernel may reach another device: no remote copies, remote signals or barrier semaphores. Data moves between devices by JAX's collectives and lax.ppermute only.
A program may use at most 128 MiB of HBM per device.

v0:
```python
import jax
import jax.numpy as jnp
from jax import lax
from jax.sharding import PartitionSpec as P

ALL = ("depth", "row", "col")
BF = jnp.bfloat16
F32 = jnp.float32


def place(y, x, z, core):
    x, y, z = x % 4, y % 4, z % 4
    return (y * 8 + (x % 2) * 4 + z) * 4 + (x // 2) * 2 + core


def pull(a, source):
    pairs = []
    for y in range(4):
        for x in range(4):
            for z in range(4):
                for core in range(2):
                    pairs.append((place(*source(y, x, z, core)), place(y, x, z, core)))
    return lax.ppermute(a, ALL, pairs)


def near(a, k):
    return pull(a, lambda y, x, z, c: (y, x + k * c, z + k * (1 - c), c))


def far(a, k):
    return pull(a, lambda y, x, z, c: (y, x + k * (1 - c), z + k * c, c))


def from_y(a, k):
    return pull(a, lambda y, x, z, c: (y + k, x, z, c))


def other_core(a):
    return pull(a, lambda y, x, z, c: (y, x, z, 1 - c))


def outer(left, right):
    return lax.dot_general(left, right, (((1,), (1,)), ((), ())), preferred_element_type=F32)


def inner(left, right):
    return lax.dot_general(left, right, (((0,), (0,)), ((), ())), preferred_element_type=F32)


def dot(left, right):
    return jnp.dot(left, right, preferred_element_type=F32)


def cat(*parts, axis=0):
    return jnp.concatenate(parts, axis=axis)


def together(*arrays):
    return lax.optimization_barrier(arrays)


def blocks_of(parts):
    n = parts[0].shape[0] // 96
    return lambda k: cat(*[p.reshape(n, 4, 24, 896)[:, k] for p in parts], axis=2).reshape(n * 24, 2688)


def first_step(block):
    across = block(2).astype(BF)
    half = across.shape[0] // 2
    return from_y(across[:half], -1), from_y(across[half:], 1)


def second_step(block, via_up, via_down):
    half = via_up.shape[0]
    up, down = block(1), block(3)
    up = cat((up[:half] + via_up.astype(F32)).astype(BF), up[half:].astype(BF))
    down = cat(down[:half].astype(BF), (down[half:] + via_down.astype(F32)).astype(BF))
    return up, down


def last_step(block, up, down):
    return block(0) + from_y(up, -1).astype(F32) + from_y(down, 1).astype(F32)


def by_row(*blocks):
    rows, width = blocks[0].shape
    return cat(*[b.reshape(rows // 24, 1, 24, width) for b in blocks], axis=1).reshape(rows * 4, width)


def pointwise(total):
    gate, up, hidden_grad = total[:, :896], total[:, 896:1792], total[:, 1792:]
    sigma = jax.nn.sigmoid(gate)
    active = gate * sigma
    hidden = (active * up).astype(BF)
    gate_delta = (hidden_grad * up * sigma * (1.0 + gate * (1.0 - sigma))).astype(BF)
    up_delta = (hidden_grad * active).astype(BF)
    return cat(hidden, gate_delta, up_delta, axis=1)


def spread(a):
    return from_y(a, -1), from_y(a, 1)


def spread_across(before, after):
    half = before.shape[0] // 2
    return cat(from_y(before[:half], -1), from_y(after[half:], 1))


def body(tokens, cotangent, gate_weight, up_weight, down_weight):
    y = lax.axis_index("depth")
    width = tokens.shape[1]

    def products(tok, cot):
        return [dot(tok, gate_weight), dot(tok, up_weight), outer(cot, down_weight)]

    def back_products(delta):
        return outer(delta[:, :896], gate_weight) + outer(delta[:, 896:], up_weight)

    tc = cat(tokens, cotangent)
    first = jnp.zeros((2, 4, 24, width), BF)
    for k, b in ((0, tc), (1, near(tc, 1)), (3, near(tc, 3)), (2, near(tc, 2))):
        first = lax.dynamic_update_slice_in_dim(first, b.reshape(2, 1, 24, width), lax.rem(k - y + 4, 4), 1)
    q0 = first.reshape(2, 96, width)
    q1, q3, q2 = far(q0, 1), far(q0, 3), far(q0, 2)
    qa = cat(q0, q1, q3, q2, axis=1)
    qb = other_core(qa)

    block_a = blocks_of(products(*qa))
    via_a = first_step(block_a)
    *part_b, via_up, via_down = together(*products(*qb), *via_a)
    block_b = blocks_of(part_b)
    via_b = first_step(block_b)
    up_a, down_a = second_step(block_a, via_up, via_down)
    up_b, down_b = second_step(block_b, *via_b)
    own = pointwise(last_step(block_a, up_a, down_a))
    other = pointwise(last_step(block_b, up_b, down_b))

    delta, hidden = cat(own[:, 896:], other[:, 896:]), cat(own[:, :896], other[:, :896])
    before_d, after_d, before_h, after_h = together(*spread(delta), *spread(hidden))
    across_d = spread_across(before_d, after_d)
    across_h = spread_across(before_h, after_h)
    delta = by_row(delta, after_d, across_d, before_d)
    hidden = by_row(hidden, after_h, across_h, before_h)

    part_other = other_core(back_products(delta[384:]))
    part = back_products(delta[:384]) + part_other
    part_bf, delta = together(part.astype(BF), delta)
    tok, cot = cat(qa[0], qb[0]), cat(qa[1], qb[1])
    gate_grad = inner(tok, delta[:, :896]).astype(BF)
    up_grad = inner(tok, delta[:, 896:]).astype(BF)
    gate_grad, up_grad, *parts = together(
        gate_grad, up_grad, *[far(part_bf[96 * n : 96 * n + 96], -k) for n, k in ((1, 1), (2, 3), (3, 2))]
    )
    total = part[:96] + sum(p.astype(F32) for p in parts)
    total, hidden = together(total, hidden)
    down_grad = inner(hidden, cot).astype(BF)

    def block(k):
        return lax.dynamic_slice_in_dim(total, lax.rem(k - y + 4, 4) * 24, 24, 0)

    tokens_grad = block(0) + sum(near(block(k), -k) for k in (1, 3, 2))
    return tokens_grad.astype(BF), gate_grad, up_grad, down_grad


def solution(mesh):
    act, weight, turned = P(("row", "col"), "depth"), P("depth", ("row", "col")), P(("row", "col"), "depth")
    return jax.shard_map(
        body, mesh=mesh, in_specs=(act, act, weight, weight, turned), out_specs=(act, weight, weight, turned), check_vma=False
    )
```

profile of v0, /device:TPU:0, one launch (start us, length us, event | category | flops | bytes accessed | tf_op | source)
XLA Modules:
  0.0 175.8 jit_solution(2003822471276062018)
XLA Ops:
  2.4 4.0 %collective-permute-start.2 = (bf16[48,2048]{1,0:T(8,128)(2,1)S(1)}, bf16[48,2048]{1,0:T(8,128)(2,1)S(1)}, u32[]{:S(2)}, u32[]{:S(2)}) collective-permute-start(bf16[48,2048]{1,0:T(8,128)(2,1)S(1)} %constant_dynamic-update-slice_fusion), channel_id=1, source_target_pairs={{8,0},{3,1},{12,4},{7,5},{0,8},{11,9},{4,12},{15,13},{24,16},{19,1... | collective-permute-start | bytes 589832 | tf_op jit(solution)/shard_map/ppermute | solution.py:23
  9.7 3.4 %collective-permute-done = bf16[48,2048]{1,0:T(8,128)(2,1)S(1)} collective-permute-done((bf16[48,2048]{1,0:T(8,128)(2,1)S(1)}, bf16[48,2048]{1,0:T(8,128)(2,1)S(1)}, u32[]{:S(2)}, u32[]{:S(2)}) %collective-permute-start) | collective-permute-done | bytes 196640 | tf_op jit(solution)/shard_map/ppermute | solution.py:23
  13.3 3.1 %collective-permute-start.5 = (bf16[2,96,2048]{2,1,0:T(8,128)(2,1)S(1)}, bf16[2,96,2048]{2,1,0:T(8,128)(2,1)S(1)}, u32[]{:S(2)}, u32[]{:S(2)}) collective-permute-start(bf16[2,96,2048]{2,1,0:T(8,128)(2,1)S(1)} %bitcast.141), channel_id=1, source_target_pairs={{2,0},{9,1},{6,4},{13,5},{10,8},{1,9},{14,12},{5,13},{18,16},{25,1... | collective-permute-start | bytes 2359304 | tf_op jit(solution)/shard_map/ppermute | solution.py:23
  19.7 7.3 %collective-permute-done.5 = bf16[2,96,2048]{2,1,0:T(8,128)(2,1)S(1)} collective-permute-done((bf16[2,96,2048]{2,1,0:T(8,128)(2,1)S(1)}, bf16[2,96,2048]{2,1,0:T(8,128)(2,1)S(1)}, u32[]{:S(2)}, u32[]{:S(2)}) %collective-permute-start.5) | collective-permute-done | bytes 786464 | tf_op jit(solution)/shard_map/ppermute | solution.py:23
  27.0 8.3 %collective-permute-done.4 = bf16[2,96,2048]{2,1,0:T(8,128)(2,1)S(1)} collective-permute-done((bf16[2,96,2048]{2,1,0:T(8,128)(2,1)S(1)}, bf16[2,96,2048]{2,1,0:T(8,128)(2,1)S(1)}, u32[]{:S(2)}, u32[]{:S(2)}) %collective-permute-start.4) | collective-permute-done | bytes 786464 | tf_op jit(solution)/shard_map/ppermute | solution.py:23
  44.9 3.1 %collective-permute-start.8 = (bf16[48,2688]{1,0:T(8,128)(2,1)S(1)}, bf16[48,2688]{1,0:T(8,128)(2,1)S(1)}, u32[]{:S(2)}, u32[]{:S(2)}) collective-permute-start(bf16[48,2688]{1,0:T(8,128)(2,1)S(1)} %get-tuple-element.80), channel_id=1, source_target_pairs={{32,0},{33,1},{36,4},{37,5},{40,8},{41,9},{44,12},{45,13},{48,16},... | collective-permute-start | bytes 774152 | tf_op jit(solution)/shard_map/ppermute | solution.py:23
  54.0 3.4 %collective-permute-done.7 = bf16[48,2688]{1,0:T(8,128)(2,1)S(1)} collective-permute-done((bf16[48,2688]{1,0:T(8,128)(2,1)S(1)}, bf16[48,2688]{1,0:T(8,128)(2,1)S(1)}, u32[]{:S(2)}, u32[]{:S(2)}) %collective-permute-start.7) | collective-permute-done | bytes 258080 | tf_op jit(solution)/shard_map/ppermute | solution.py:23
  59.0 3.2 %collective-permute-start.13 = (bf16[48,2688]{1,0:T(8,128)(2,1)S(1)}, bf16[48,2688]{1,0:T(8,128)(2,1)S(1)}, u32[]{:S(2)}, u32[]{:S(2)}) collective-permute-start(bf16[48,2688]{1,0:T(8,128)(2,1)S(1)} %get-tuple-element.79), channel_id=1, source_target_pairs={{32,0},{33,1},{36,4},{37,5},{40,8},{41,9},{44,12},{45,13},{48,16},... | collective-permute-start | bytes 774152 | tf_op jit(solution)/shard_map/ppermute | solution.py:23
  64.6 4.7 %collective-permute-done.11 = bf16[48,2688]{1,0:T(8,128)(2,1)S(1)} collective-permute-done((bf16[48,2688]{1,0:T(8,128)(2,1)S(1)}, bf16[48,2688]{1,0:T(8,128)(2,1)S(1)}, u32[]{:S(2)}, u32[]{:S(2)}) %collective-permute-start.11) | collective-permute-done | bytes 258080 | tf_op jit(solution)/shard_map/ppermute | solution.py:23
  69.7 3.3 %collective-permute-start.14 = (bf16[96,2688]{1,0:T(8,128)(2,1)S(1)}, bf16[96,2688]{1,0:T(8,128)(2,1)S(1)}, u32[]{:S(2)}, u32[]{:S(2)}) collective-permute-start(bf16[96,2688]{1,0:T(8,128)(2,1)S(1)} %pad_maximum_fusion.16), channel_id=1, source_target_pairs={{32,0},{33,1},{36,4},{37,5},{40,8},{41,9},{44,12},{45,13},{48,16},... | collective-permute-start | bytes 1548296 | tf_op jit(solution)/shard_map/ppermute | solution.py:23
  73.0 7.0 %collective-permute-done.10 = bf16[96,2688]{1,0:T(8,128)(2,1)S(1)} collective-permute-done((bf16[96,2688]{1,0:T(8,128)(2,1)S(1)}, bf16[96,2688]{1,0:T(8,128)(2,1)S(1)}, u32[]{:S(2)}, u32[]{:S(2)}) %collective-permute-start.10) | collective-permute-done | bytes 516128 | tf_op jit(solution)/shard_map/ppermute | solution.py:23
  80.8 8.9 %collective-permute-done.12 = bf16[96,2688]{1,0:T(8,128)(2,1)S(1)} collective-permute-done((bf16[96,2688]{1,0:T(8,128)(2,1)S(1)}, bf16[96,2688]{1,0:T(8,128)(2,1)S(1)}, u32[]{:S(2)}, u32[]{:S(2)}) %collective-permute-start.12) | collective-permute-done | bytes 516128 | tf_op jit(solution)/shard_map/ppermute | solution.py:23
  93.2 3.3 %collective-permute-start.18 = (bf16[192,896]{1,0:T(8,128)(2,1)S(1)}, bf16[192,896]{1,0:T(8,128)(2,1)S(1)}, u32[]{:S(2)}, u32[]{:S(2)}) collective-permute-start(bf16[192,896]{1,0:T(8,128)(2,1)S(1)} %pad_maximum_fusion.17), channel_id=1, source_target_pairs={{32,0},{33,1},{36,4},{37,5},{40,8},{41,9},{44,12},{45,13},{48,16},... | collective-permute-start | bytes 1032200 | tf_op jit(solution)/shard_map/ppermute | solution.py:23
  96.5 16.9 %collective-permute-done.18 = bf16[192,896]{1,0:T(8,128)(2,1)S(1)} collective-permute-done((bf16[192,896]{1,0:T(8,128)(2,1)S(1)}, bf16[192,896]{1,0:T(8,128)(2,1)S(1)}, u32[]{:S(2)}, u32[]{:S(2)}) %collective-permute-start.18) | collective-permute-done | bytes 344096 | tf_op jit(solution)/shard_map/ppermute | solution.py:23
  113.4 3.4 %collective-permute-done.17 = bf16[192,896]{1,0:T(8,128)(2,1)S(1)} collective-permute-done((bf16[192,896]{1,0:T(8,128)(2,1)S(1)}, bf16[192,896]{1,0:T(8,128)(2,1)S(1)}, u32[]{:S(2)}, u32[]{:S(2)}) %collective-permute-start.17) | collective-permute-done | bytes 344096 | tf_op jit(solution)/shard_map/ppermute | solution.py:23
  117.0 3.2 %collective-permute-start.20 = (bf16[96,1792]{1,0:T(8,128)(2,1)S(1)}, bf16[96,1792]{1,0:T(8,128)(2,1)S(1)}, u32[]{:S(2)}, u32[]{:S(2)}) collective-permute-start(bf16[96,1792]{1,0:T(8,128)(2,1)S(1)} %slice.257), channel_id=1, source_target_pairs={{32,0},{33,1},{36,4},{37,5},{40,8},{41,9},{44,12},{45,13},{48,16},... | collective-permute-start | bytes 1032200 | tf_op jit(solution)/shard_map/ppermute | solution.py:23
  120.2 5.2 %collective-permute-done.19 = bf16[96,1792]{1,0:T(8,128)(2,1)S(1)} collective-permute-done((bf16[96,1792]{1,0:T(8,128)(2,1)S(1)}, bf16[96,1792]{1,0:T(8,128)(2,1)S(1)}, u32[]{:S(2)}, u32[]{:S(2)}) %collective-permute-start.19) | collective-permute-done | bytes 344096 | tf_op jit(solution)/shard_map/ppermute | solution.py:23
  129.0 3.5 %convolution_add_fusion = f32[384,2048]{1,0:T(8,128)} fusion(f32[384,2048]{1,0:T(8,128)S(1)} %fusion.14, bf16[2048,896]{1,0:T(8,128)(2,1)S(1)} %copy-done, bf16[384,1792]{1,0:T(8,128)(2,1)S(1)} %bitcast.156), kind=kOutput, calls=%fused_computation.15 | convolution fusion | flops 1410072576 | bytes 10649600 | tf_op jit(solution)/shard_map/dot_general | solution.py:43
  133.6 3.3 %collective-permute-start.26 = (bf16[96,896]{1,0:T(8,128)(2,1)S(1)}, bf16[96,896]{1,0:T(8,128)(2,1)S(1)}, u32[]{:S(2)}, u32[]{:S(2)}) collective-permute-start(bf16[96,896]{1,0:T(8,128)(2,1)S(1)} %slice.273), channel_id=1, source_target_pairs={{32,0},{33,1},{36,4},{37,5},{40,8},{41,9},{44,12},{45,13},{48,16},... | collective-permute-start | bytes 516104 | tf_op jit(solution)/shard_map/ppermute | solution.py:23
  144.2 4.0 %fusion.35 = (bf16[384,2048]{1,0:T(8,128)(2,1)S(1)}, f32[384,2048]{1,0:T(8,128)S(1)}) fusion(f32[384,2048]{1,0:T(8,128)} %collective-permute-done.21, f32[384,2048]{1,0:T(8,128)S(1)} %fusion.17, bf16[2048,896]{1,0:T(8,128)(2,1)S(1)} %copy-done.1, bf16[384,1792]{1,0:T(8,128)(2,1)S(1)} %bitcast.146), kind=kOutput, calls=%fused_computation.109 | convolution fusion | flops 1411645440 | bytes 15368192 | tf_op jit(solution)/shard_map/dot_general | solution.py:43
  152.7 5.0 %convolution_convert_fusion.1 = bf16[2048,896]{1,0:T(8,128)(2,1)} fusion(bf16[384,2048]{1,0:T(8,128)(2,1)S(1)} %get-tuple-element.45, bf16[384,2048]{1,0:T(8,128)(2,1)S(1)} %copy-done.7, bf16[768,1792]{1,0:T(8,128)(2,1)S(1)} %bitcast.139), kind=kOutput, calls=%fused_computation.7 | convolution fusion | flops 2826698752 | bytes 8192000 | tf_op jit(solution)/shard_map/dot_general | solution.py:47
  157.6 5.0 %convolution_convert_fusion.2 = bf16[2048,896]{1,0:T(8,128)(2,1)} fusion(bf16[384,2048]{1,0:T(8,128)(2,1)S(1)} %get-tuple-element.45, bf16[384,2048]{1,0:T(8,128)(2,1)S(1)} %copy-done.7, bf16[768,1792]{1,0:T(8,128)(2,1)S(1)} %bitcast.140), kind=kOutput, calls=%fused_computation.8 | convolution fusion | flops 2826698752 | bytes 8192000 | tf_op jit(solution)/shard_map/dot_general | solution.py:47
  162.9 3.3 %collective-permute-start.28 = (f32[24,2048]{1,0:T(8,128)S(1)}, f32[24,2048]{1,0:T(8,128)S(1)}, u32[]{:S(2)}, u32[]{:S(2)}) collective-permute-start(f32[24,2048]{1,0:T(8,128)S(1)} %get-tuple-element.75), channel_id=1, source_target_pairs={{4,0},{17,1},{8,4},{21,5},{12,8},{25,9},{0,12},{29,13},{20,16},{3,... | collective-permute-start | bytes 589832 | tf_op jit(solution)/shard_map/ppermute | solution.py:23
  167.1 4.5 %convolution_convert_fusion = bf16[896,2048]{1,0:T(8,128)(2,1)} fusion(bf16[768,896]{1,0:T(8,128)(2,1)S(1)} %bitcast.154, bf16[384,2048]{1,0:T(8,128)(2,1)S(1)} %get-tuple-element.44, bf16[384,2048]{1,0:T(8,128)(2,1)S(1)} %copy-done.6), kind=kOutput, calls=%fused_computation.6 | convolution fusion | flops 2826698752 | bytes 8192000 | tf_op jit(solution)/shard_map/dot_general | solution.py:47
  (140 shorter events, 54.1 us)
Async XLA Ops:
  2.4 10.9 %collective-permute-start.2 = (bf16[48,2048]{1,0:T(8,128)(2,1)S(1)}, bf16[48,2048]{1,0:T(8,128)(2,1)S(1)}, u32[]{:S(2)}, u32[]{:S(2)}) collective-permute-start(bf16[48,2048]{1,0:T(8,128)(2,1)S(1)} %constant_dynamic-update-slice_fusion), channel_id=1, source_target_pairs={{8,0},{3,1},{12,4},{7,5},{0,8},{11,9},{4,12},{15,13},{24,16},{19,1... | collective-permute-start | bytes 589832 | tf_op jit(solution)/shard_map/ppermute | solution.py:23
  13.3 13.7 %collective-permute-start.5 = (bf16[2,96,2048]{2,1,0:T(8,128)(2,1)S(1)}, bf16[2,96,2048]{2,1,0:T(8,128)(2,1)S(1)}, u32[]{:S(2)}, u32[]{:S(2)}) collective-permute-start(bf16[2,96,2048]{2,1,0:T(8,128)(2,1)S(1)} %bitcast.141), channel_id=1, source_target_pairs={{2,0},{9,1},{6,4},{13,5},{10,8},{1,9},{14,12},{5,13},{18,16},{25,1... | collective-permute-start | bytes 2359304 | tf_op jit(solution)/shard_map/ppermute | solution.py:23
  16.4 18.9 %collective-permute-start.4 = (bf16[2,96,2048]{2,1,0:T(8,128)(2,1)S(1)}, bf16[2,96,2048]{2,1,0:T(8,128)(2,1)S(1)}, u32[]{:S(2)}, u32[]{:S(2)}) collective-permute-start(bf16[2,96,2048]{2,1,0:T(8,128)(2,1)S(1)} %bitcast.142), channel_id=1, source_target_pairs={{18,0},{13,1},{22,4},{1,5},{26,8},{5,9},{30,12},{9,13},{0,16},{29,... | collective-permute-start | bytes 2359304 | tf_op jit(solution)/shard_map/ppermute | solution.py:23
  17.0 18.4 %collective-permute-start.3 = (bf16[2,96,2048]{2,1,0:T(8,128)(2,1)S(1)}, bf16[2,96,2048]{2,1,0:T(8,128)(2,1)S(1)}, u32[]{:S(2)}, u32[]{:S(2)}) collective-permute-start(bf16[2,96,2048]{2,1,0:T(8,128)(2,1)S(1)} %bitcast.143), channel_id=1, source_target_pairs={{16,0},{5,1},{20,4},{9,5},{24,8},{13,9},{28,12},{1,13},{2,16},{21,... | collective-permute-start | bytes 2359304 | tf_op jit(solution)/shard_map/ppermute | solution.py:23
  35.7 12.3 %collective-permute-start.6 = (bf16[2,384,2048]{2,1,0:T(8,128)(2,1)S(1)}, bf16[2,384,2048]{2,1,0:T(8,128)(2,1)S(1)}, u32[]{:S(2)}, u32[]{:S(2)}) collective-permute-start(bf16[2,384,2048]{2,1,0:T(8,128)(2,1)S(1)} %pad_maximum_fusion), channel_id=1, source_target_pairs={{1,0},{0,1},{5,4},{4,5},{9,8},{8,9},{13,12},{12,13},{17,16},{16,17... | collective-permute-start | bytes 9437192 | tf_op jit(solution)/shard_map/ppermute | solution.py:23
  44.9 9.1 %collective-permute-start.8 = (bf16[48,2688]{1,0:T(8,128)(2,1)S(1)}, bf16[48,2688]{1,0:T(8,128)(2,1)S(1)}, u32[]{:S(2)}, u32[]{:S(2)}) collective-permute-start(bf16[48,2688]{1,0:T(8,128)(2,1)S(1)} %get-tuple-element.80), channel_id=1, source_target_pairs={{32,0},{33,1},{36,4},{37,5},{40,8},{41,9},{44,12},{45,13},{48,16},... | collective-permute-start | bytes 774152 | tf_op jit(solution)/shard_map/ppermute | solution.py:23
  48.0 9.4 %collective-permute-start.7 = (bf16[48,2688]{1,0:T(8,128)(2,1)S(1)}, bf16[48,2688]{1,0:T(8,128)(2,1)S(1)}, u32[]{:S(2)}, u32[]{:S(2)}) collective-permute-start(bf16[48,2688]{1,0:T(8,128)(2,1)S(1)} %get-tuple-element.81), channel_id=1, source_target_pairs={{96,0},{97,1},{100,4},{101,5},{104,8},{105,9},{108,12},{109,13},{1... | collective-permute-start | bytes 774152 | tf_op jit(solution)/shard_map/ppermute | solution.py:23
  58.9 10.4 %collective-permute-start.11 = (bf16[48,2688]{1,0:T(8,128)(2,1)S(1)}, bf16[48,2688]{1,0:T(8,128)(2,1)S(1)}, u32[]{:S(2)}, u32[]{:S(2)}) collective-permute-start(bf16[48,2688]{1,0:T(8,128)(2,1)S(1)} %get-tuple-element.78), channel_id=1, source_target_pairs={{96,0},{97,1},{100,4},{101,5},{104,8},{105,9},{108,12},{109,13},{1... | collective-permute-start | bytes 774152 | tf_op jit(solution)/shard_map/ppermute | solution.py:23
  59.0 10.6 %collective-permute-start.13 = (bf16[48,2688]{1,0:T(8,128)(2,1)S(1)}, bf16[48,2688]{1,0:T(8,128)(2,1)S(1)}, u32[]{:S(2)}, u32[]{:S(2)}) collective-permute-start(bf16[48,2688]{1,0:T(8,128)(2,1)S(1)} %get-tuple-element.79), channel_id=1, source_target_pairs={{32,0},{33,1},{36,4},{37,5},{40,8},{41,9},{44,12},{45,13},{48,16},... | collective-permute-start | bytes 774152 | tf_op jit(solution)/shard_map/ppermute | solution.py:23
  62.4 17.6 %collective-permute-start.10 = (bf16[96,2688]{1,0:T(8,128)(2,1)S(1)}, bf16[96,2688]{1,0:T(8,128)(2,1)S(1)}, u32[]{:S(2)}, u32[]{:S(2)}) collective-permute-start(bf16[96,2688]{1,0:T(8,128)(2,1)S(1)} %pad_maximum_fusion.13), channel_id=1, source_target_pairs={{32,0},{33,1},{36,4},{37,5},{40,8},{41,9},{44,12},{45,13},{48,16},... | collective-permute-start | bytes 1548296 | tf_op jit(solution)/shard_map/ppermute | solution.py:23
  62.6 17.9 %collective-permute-start.9 = (bf16[96,2688]{1,0:T(8,128)(2,1)S(1)}, bf16[96,2688]{1,0:T(8,128)(2,1)S(1)}, u32[]{:S(2)}, u32[]{:S(2)}) collective-permute-start(bf16[96,2688]{1,0:T(8,128)(2,1)S(1)} %pad_maximum_fusion.12), channel_id=1, source_target_pairs={{96,0},{97,1},{100,4},{101,5},{104,8},{105,9},{108,12},{109,13},{1... | collective-permute-start | bytes 1548296 | tf_op jit(solution)/shard_map/ppermute | solution.py:23
  69.5 20.2 %collective-permute-start.12 = (bf16[96,2688]{1,0:T(8,128)(2,1)S(1)}, bf16[96,2688]{1,0:T(8,128)(2,1)S(1)}, u32[]{:S(2)}, u32[]{:S(2)}) collective-permute-start(bf16[96,2688]{1,0:T(8,128)(2,1)S(1)} %pad_maximum_fusion.15), channel_id=1, source_target_pairs={{96,0},{97,1},{100,4},{101,5},{104,8},{105,9},{108,12},{109,13},{1... | collective-permute-start | bytes 1548296 | tf_op jit(solution)/shard_map/ppermute | solution.py:23
  69.7 20.0 %collective-permute-start.14 = (bf16[96,2688]{1,0:T(8,128)(2,1)S(1)}, bf16[96,2688]{1,0:T(8,128)(2,1)S(1)}, u32[]{:S(2)}, u32[]{:S(2)}) collective-permute-start(bf16[96,2688]{1,0:T(8,128)(2,1)S(1)} %pad_maximum_fusion.16), channel_id=1, source_target_pairs={{32,0},{33,1},{36,4},{37,5},{40,8},{41,9},{44,12},{45,13},{48,16},... | collective-permute-start | bytes 1548296 | tf_op jit(solution)/shard_map/ppermute | solution.py:23
  90.1 26.7 %collective-permute-start.16 = (bf16[192,1792]{1,0:T(8,128)(2,1)S(1)}, bf16[192,1792]{1,0:T(8,128)(2,1)S(1)}, u32[]{:S(2)}, u32[]{:S(2)}) collective-permute-start(bf16[192,1792]{1,0:T(8,128)(2,1)S(1)} %maximum_maximum_fusion), channel_id=1, source_target_pairs={{32,0},{33,1},{36,4},{37,5},{40,8},{41,9},{44,12},{45,13},{48,16},... | collective-permute-start | bytes 2064392 | tf_op jit(solution)/shard_map/ppermute | solution.py:23
  93.2 23.7 %collective-permute-start.15 = (bf16[192,1792]{1,0:T(8,128)(2,1)S(1)}, bf16[192,1792]{1,0:T(8,128)(2,1)S(1)}, u32[]{:S(2)}, u32[]{:S(2)}) collective-permute-start(bf16[192,1792]{1,0:T(8,128)(2,1)S(1)} %maximum_maximum_fusion), channel_id=1, source_target_pairs={{96,0},{97,1},{100,4},{101,5},{104,8},{105,9},{108,12},{109,13},{1... | collective-permute-start | bytes 2064392 | tf_op jit(solution)/shard_map/ppermute | solution.py:23
  93.2 20.2 %collective-permute-start.18 = (bf16[192,896]{1,0:T(8,128)(2,1)S(1)}, bf16[192,896]{1,0:T(8,128)(2,1)S(1)}, u32[]{:S(2)}, u32[]{:S(2)}) collective-permute-start(bf16[192,896]{1,0:T(8,128)(2,1)S(1)} %pad_maximum_fusion.17), channel_id=1, source_target_pairs={{32,0},{33,1},{36,4},{37,5},{40,8},{41,9},{44,12},{45,13},{48,16},... | collective-permute-start | bytes 1032200 | tf_op jit(solution)/shard_map/ppermute | solution.py:23
  96.5 20.3 %collective-permute-start.17 = (bf16[192,896]{1,0:T(8,128)(2,1)S(1)}, bf16[192,896]{1,0:T(8,128)(2,1)S(1)}, u32[]{:S(2)}, u32[]{:S(2)}) collective-permute-start(bf16[192,896]{1,0:T(8,128)(2,1)S(1)} %pad_maximum_fusion.17), channel_id=1, source_target_pairs={{96,0},{97,1},{100,4},{101,5},{104,8},{105,9},{108,12},{109,13},{1... | collective-permute-start | bytes 1032200 | tf_op jit(solution)/shard_map/ppermute | solution.py:23
  116.9 8.5 %collective-permute-start.19 = (bf16[96,1792]{1,0:T(8,128)(2,1)S(1)}, bf16[96,1792]{1,0:T(8,128)(2,1)S(1)}, u32[]{:S(2)}, u32[]{:S(2)}) collective-permute-start(bf16[96,1792]{1,0:T(8,128)(2,1)S(1)} %slice.256), channel_id=1, source_target_pairs={{96,0},{97,1},{100,4},{101,5},{104,8},{105,9},{108,12},{109,13},{1... | collective-permute-start | bytes 1032200 | tf_op jit(solution)/shard_map/ppermute | solution.py:23
  132.5 11.4 %collective-permute-start.21 = (f32[384,2048]{1,0:T(8,128)}, f32[384,2048]{1,0:T(8,128)}, u32[]{:S(2)}, u32[]{:S(2)}) collective-permute-start(f32[384,2048]{1,0:T(8,128)} %convolution_add_fusion), channel_id=1, source_target_pairs={{1,0},{0,1},{5,4},{4,5},{9,8},{8,9},{13,12},{12,13},{17,16},{16,17... | collective-permute-start | bytes 9437192 | tf_op jit(solution)/shard_map/ppermute | solution.py:23
  148.3 14.3 %collective-permute-start.24 = (bf16[96,2048]{1,0:T(8,128)(2,1)S(1)}, bf16[96,2048]{1,0:T(8,128)(2,1)S(1)}, u32[]{:S(2)}, u32[]{:S(2)}) collective-permute-start(bf16[96,2048]{1,0:T(8,128)(2,1)S(1)} %get-tuple-element.48), channel_id=1, source_target_pairs={{2,0},{9,1},{6,4},{13,5},{10,8},{1,9},{14,12},{5,13},{18,16},{25,1... | collective-permute-start | bytes 1179656 | tf_op jit(solution)/shard_map/ppermute | solution.py:23
  150.3 12.3 %collective-permute-start.23 = (bf16[96,2048]{1,0:T(8,128)(2,1)S(1)}, bf16[96,2048]{1,0:T(8,128)(2,1)S(1)}, u32[]{:S(2)}, u32[]{:S(2)}) collective-permute-start(bf16[96,2048]{1,0:T(8,128)(2,1)S(1)} %get-tuple-element.49), channel_id=1, source_target_pairs={{16,0},{5,1},{20,4},{9,5},{24,8},{13,9},{28,12},{1,13},{2,16},{21,... | collective-permute-start | bytes 1179656 | tf_op jit(solution)/shard_map/ppermute | solution.py:23
  152.7 9.9 %collective-permute-start.22 = (bf16[96,2048]{1,0:T(8,128)(2,1)S(1)}, bf16[96,2048]{1,0:T(8,128)(2,1)S(1)}, u32[]{:S(2)}, u32[]{:S(2)}) collective-permute-start(bf16[96,2048]{1,0:T(8,128)(2,1)S(1)} %get-tuple-element.50), channel_id=1, source_target_pairs={{18,0},{13,1},{22,4},{1,5},{26,8},{5,9},{30,12},{9,13},{0,16},{29,... | collective-permute-start | bytes 1179656 | tf_op jit(solution)/shard_map/ppermute | solution.py:23
  162.9 8.8 %collective-permute-start.28 = (f32[24,2048]{1,0:T(8,128)S(1)}, f32[24,2048]{1,0:T(8,128)S(1)}, u32[]{:S(2)}, u32[]{:S(2)}) collective-permute-start(f32[24,2048]{1,0:T(8,128)S(1)} %get-tuple-element.75), channel_id=1, source_target_pairs={{4,0},{17,1},{8,4},{21,5},{12,8},{25,9},{0,12},{29,13},{20,16},{3,... | collective-permute-start | bytes 589832 | tf_op jit(solution)/shard_map/ppermute | solution.py:23
  166.2 9.0 %collective-permute-start.27 = (f32[24,2048]{1,0:T(8,128)S(1)}, f32[24,2048]{1,0:T(8,128)S(1)}, u32[]{:S(2)}, u32[]{:S(2)}) collective-permute-start(f32[24,2048]{1,0:T(8,128)S(1)} %get-tuple-element.77), channel_id=1, source_target_pairs={{12,0},{19,1},{0,4},{23,5},{4,8},{27,9},{8,12},{31,13},{28,16},{1,... | collective-permute-start | bytes 589832 | tf_op jit(solution)/shard_map/ppermute | solution.py:23
  (21 other events, 118.8 us)
where the time goes:
time: 177 us; the launch traced here: 176 us
  waiting for transfers between devices  76.2 us (43%)
  starting transfers between devices  47.2 us (27%)
  matrix products  36.4 us (21%)
  local copies, waits for them, and re-layouts  11.4 us (6%)
  other arithmetic  3.32 us (2%)
    ppermute x30, waiting for transfers between devices, pull(): return lax.ppermute(a, ALL, pairs)  76.2 us
    ppermute x30, starting transfers between devices, pull(): return lax.ppermute(a, ALL, pairs)  47.2 us
    dot_general x6, matrix products, outer(): lax.dot_general(left, right, (((1,), (1,)), ((), ())), preferred_element_...  14.8 us
    dot_general x3, matrix products, inner(): lax.dot_general(left, right, (((0,), (0,)), ((), ())), preferred_element_...  14.5 us
    dot_general x4, matrix products, dot(): return jnp.dot(left, right, preferred_element_type=F32)  7.18 us
  transfers between devices with their start and end apart: 30, of which 17 were waited for; matrix products, arithmetic and copies ran while one was open for 20% of the time, Pallas kernels for 0%

commit v1 on v0

--- a/solution.py
+++ b/solution.py
@@ -61,12 +61,12 @@
 
 def blocks_of(parts):
     n = parts[0].shape[0] // 96
-    return lambda k: cat(*[p.reshape(n, 4, 24, 896)[:, k] for p in parts], axis=2).reshape(n * 24, 2688)
+    return lambda k: cat(*[p.reshape(n, 4, 24, -1)[:, k] for p in parts], axis=2).reshape(n * 24, 2688)
 
 
 def first_step(block):
     across = block(2).astype(BF)
-    half = across.shape[0] // 2
+    half = (across.shape[0] // 2 + 7) // 8 * 8
     return from_y(across[:half], -1), from_y(across[half:], 1)
 
 
@@ -111,45 +111,56 @@
     width = tokens.shape[1]
 
     def products(tok, cot):
-        return [dot(tok, gate_weight), dot(tok, up_weight), outer(cot, down_weight)]
-
-    def back_products(delta):
-        return outer(delta[:, :896], gate_weight) + outer(delta[:, 896:], up_weight)
+        return [dot(tok, weights), outer(cot, down_weight)]
 
     tc = cat(tokens, cotangent)
+    weights = cat(gate_weight, up_weight, axis=1)
+    near_2, near_1, near_3, weights = together(near(tc, 2), near(tc, 1), near(tc, 3), weights)
     first = jnp.zeros((2, 4, 24, width), BF)
-    for k, b in ((0, tc), (1, near(tc, 1)), (3, near(tc, 3)), (2, near(tc, 2))):
+    for k, b in ((2, near_2), (1, near_1), (3, near_3), (0, tc)):
         first = lax.dynamic_update_slice_in_dim(first, b.reshape(2, 1, 24, width), lax.rem(k - y + 4, 4), 1)
     q0 = first.reshape(2, 96, width)
-    q1, q3, q2 = far(q0, 1), far(q0, 3), far(q0, 2)
-    qa = cat(q0, q1, q3, q2, axis=1)
-    qb = other_core(qa)
+    o0 = other_core(q0)
+    q2, q1, q3 = far(q0, 2), far(q0, 1), far(q0, 3)
+    tok_0, cot_0 = cat(q0[0], o0[0]), cat(q0[1], o0[1])
+    block_0 = blocks_of(products(tok_0, cot_0))
+    up_0, down_0 = second_step(block_0, *first_step(block_0))
+    q2, q1, q3, up_0, down_0 = together(q2, q1, q3, up_0, down_0)
 
-    block_a = blocks_of(products(*qa))
+    tok_a, cot_a = [cat(*[q[n] for q in (q1, q3, q2)]) for n in range(2)]
+    tok_b, cot_b = together(other_core(tok_a), other_core(cot_a))
+    *part_a, up_0, down_0 = together(*products(tok_a, cot_a), from_y(up_0, -1), from_y(down_0, 1))
+    block_a = blocks_of(part_a)
     via_a = first_step(block_a)
-    *part_b, via_up, via_down = together(*products(*qb), *via_a)
+    part_b = products(tok_b, cot_b)
     block_b = blocks_of(part_b)
     via_b = first_step(block_b)
+    *part_b, via_up, via_down = together(*part_b, *via_a)
+    total_0 = block_0(0) + up_0.astype(F32) + down_0.astype(F32)
     up_a, down_a = second_step(block_a, via_up, via_down)
     up_b, down_b = second_step(block_b, *via_b)
-    own = pointwise(last_step(block_a, up_a, down_a))
-    other = pointwise(last_step(block_b, up_b, down_b))
+    result_0 = pointwise(total_0)
+    own = cat(result_0[:24], pointwise(last_step(block_a, up_a, down_a)))
+    other = cat(result_0[24:], pointwise(last_step(blocks_of(part_b), up_b, down_b)))
 
     delta, hidden = cat(own[:, 896:], other[:, 896:]), cat(own[:, :896], other[:, :896])
-    before_d, after_d, before_h, after_h = together(*spread(delta), *spread(hidden))
+    before_d, after_d = spread(delta)
+    before_d, after_d, hidden = together(before_d, after_d, hidden)
     across_d = spread_across(before_d, after_d)
-    across_h = spread_across(before_h, after_h)
     delta = by_row(delta, after_d, across_d, before_d)
-    hidden = by_row(hidden, after_h, across_h, before_h)
+    before_h, after_h = spread(hidden)
+    delta_own, before_h, after_h = together(delta[:384], before_h, after_h)
+    hidden = by_row(hidden, after_h, spread_across(before_h, after_h), before_h)
 
-    part_other = other_core(back_products(delta[384:]))
-    part = back_products(delta[:384]) + part_other
-    part_bf, delta = together(part.astype(BF), delta)
-    tok, cot = cat(qa[0], qb[0]), cat(qa[1], qb[1])
-    gate_grad = inner(tok, delta[:, :896]).astype(BF)
-    up_grad = inner(tok, delta[:, 896:]).astype(BF)
+    part_other = other_core(outer(delta[384:], weights).astype(BF))
+    part_own, part_other = together(outer(delta_own, weights), part_other)
+    part = part_own + part_other.astype(F32)
+    part_bf, gate_delta, up_delta = together(part.astype(BF), delta[:, :896], delta[:, 896:])
+    tok, cot = cat(tok_0[:96], tok_a, tok_0[96:], tok_b), cat(cot_0[:96], cot_a, cot_0[96:], cot_b)
+    gate_grad = inner(tok, gate_delta).astype(BF)
+    up_grad = inner(tok, up_delta).astype(BF)
     gate_grad, up_grad, *parts = together(
-        gate_grad, up_grad, *[far(part_bf[96 * n : 96 * n + 96], -k) for n, k in ((1, 1), (2, 3), (3, 2))]
+        gate_grad, up_grad, *[far(part_bf[96 * n : 96 * n + 96], -k) for n, k in ((3, 2), (1, 1), (2, 3))]
     )
     total = part[:96] + sum(p.astype(F32) for p in parts)
     total, hidden = together(total, hidden)
@@ -158,7 +169,7 @@
     def block(k):
         return lax.dynamic_slice_in_dim(total, lax.rem(k - y + 4, 4) * 24, 24, 0)
 
-    tokens_grad = block(0) + sum(near(block(k), -k) for k in (1, 3, 2))
+    tokens_grad = block(0) + sum(near(block(k), -k) for k in (2, 1, 3))
     return tokens_grad.astype(BF), gate_grad, up_grad, down_grad
 
 

time: 177 us -> 153 us (0.86)
  waiting for transfers between devices: 76.2 us -> 47.9 us
  starting transfers between devices: 47.2 us -> 54.7 us
  local copies, waits for them, and re-layouts: 11.4 us -> 3.95 us
  other arithmetic: 3.32 us -> 10.4 us
  matrix products: 36.4 us -> 34.2 us
    ppermute x30 -> x36, waiting for transfers between devices: 76.2 us -> 47.9 us  [pull(): return lax.ppermute(a, ALL, pairs)]
    ppermute x30 -> x36, starting transfers between devices: 47.2 us -> 54.7 us  [pull(): return lax.ppermute(a, ALL, pairs)]
    concatenate x16 -> x23, other arithmetic: 1.52 us -> 7.87 us  [cat(): return jnp.concatenate(parts, axis=axis)]
    another operation x2 -> x0, local copies, waits for them, and re-layouts: 4.66 us -> none  [the longest x1 2.41 us: body(): block_a = blocks_of(products(*qa))]
    dot_general x6 -> x5, matrix products: 14.8 us -> 10.3 us  [outer(): lax.dot_general(left, right, (((1,), (1,)), ((), ())), preferred_element_...]
    dot_general x4 -> x3, matrix products: 7.18 us -> 9.49 us  [dot(): return jnp.dot(left, right, preferred_element_type=F32)]
  transfers between devices with their start and end apart: 30 -> 36, of which waited for: 17 -> 13; matrix products, arithmetic and copies ran while one was open for 20% -> 27% of each run, Pallas kernels for 0% -> 0%
where the time goes in v1:
time: 153 us
  starting transfers between devices  54.7 us (36%)
  waiting for transfers between devices  47.9 us (31%)
  matrix products  34.2 us (22%)
  other arithmetic  10.4 us (7%)
  local copies, waits for them, and re-layouts  3.95 us (3%)
    ppermute x36, starting transfers between devices, pull(): return lax.ppermute(a, ALL, pairs)  54.7 us
    ppermute x36, waiting for transfers between devices, pull(): return lax.ppermute(a, ALL, pairs)  47.9 us
    dot_general x3, matrix products, inner(): lax.dot_general(left, right, (((0,), (0,)), ((), ())), preferred_element_...  14.4 us
    dot_general x5, matrix products, outer(): lax.dot_general(left, right, (((1,), (1,)), ((), ())), preferred_element_...  10.3 us
    dot_general x3, matrix products, dot(): return jnp.dot(left, right, preferred_element_type=F32)  9.49 us
    concatenate x23, other arithmetic, cat(): return jnp.concatenate(parts, axis=axis)  7.87 us
  transfers between devices with their start and end apart: 36, of which 13 were waited for; matrix products, arithmetic and copies ran while one was open for 27% of the time, Pallas kernels for 0%

profile of v1, /device:TPU:0, one launch (start us, length us, event | category | flops | bytes accessed | tf_op | source)
XLA Modules:
  0.0 152.6 jit_solution(5526472471766868248)
XLA Ops:
  2.4 4.0 %collective-permute-start = (bf16[48,2048]{1,0:T(8,128)(2,1)S(1)}, bf16[48,2048]{1,0:T(8,128)(2,1)S(1)}, u32[]{:S(2)}, u32[]{:S(2)}) collective-permute-start(bf16[48,2048]{1,0:T(8,128)(2,1)S(1)} %constant_dynamic-update-slice_fusion), channel_id=1, source_target_pairs={{8,0},{3,1},{12,4},{7,5},{0,8},{11,9},{4,12},{15,13},{24,16},{19,1... | collective-permute-start | bytes 589832 | tf_op jit(solution)/shard_map/ppermute | solution.py:23
  8.4 6.6 %pad_maximum_fusion = bf16[2048,1792]{1,0:T(8,128)(2,1)} fusion(bf16[2048,896]{1,0:T(8,128)(2,1)} %param.8, bf16[2048,896]{1,0:T(8,128)(2,1)} %param.7), kind=kLoop, calls=%fused_computation | loop fusion | flops 14680064 | bytes 14680064 | tf_op jit(solution)/shard_map/concatenate | solution.py:55
  15.3 3.1 %collective-permute-start.4 = (bf16[2,96,2048]{2,1,0:T(8,128)(2,1)S(1)}, bf16[2,96,2048]{2,1,0:T(8,128)(2,1)S(1)}, u32[]{:S(2)}, u32[]{:S(2)}) collective-permute-start(bf16[2,96,2048]{2,1,0:T(8,128)(2,1)S(1)} %bitcast.139), channel_id=1, source_target_pairs={{2,0},{9,1},{6,4},{13,5},{10,8},{1,9},{14,12},{5,13},{18,16},{25,1... | collective-permute-start | bytes 2359304 | tf_op jit(solution)/shard_map/ppermute | solution.py:23
  20.7 4.8 %fusion = f32[192,1792]{1,0:T(8,128)S(1)} fusion(bf16[2048,1792]{1,0:T(8,128)(2,1)} %pad_maximum_fusion, bf16[96,2048]{1,0:T(8,128)(2,1)S(1)} %get-tuple-element.119, bf16[96,2048]{1,0:T(8,128)(2,1)S(1)} %bitcast.166), kind=kOutput, calls=%fused_computation.11 | convolution fusion | flops 1410859008 | bytes 9502720 | tf_op jit(solution)/shard_map/dot_general | solution.py:51
  27.1 3.1 %collective-permute-start.8 = (bf16[24,2688]{1,0:T(8,128)(2,1)S(1)}, bf16[24,2688]{1,0:T(8,128)(2,1)S(1)}, u32[]{:S(2)}, u32[]{:S(2)}) collective-permute-start(bf16[24,2688]{1,0:T(8,128)(2,1)S(1)} %get-tuple-element.135), channel_id=1, source_target_pairs={{32,0},{33,1},{36,4},{37,5},{40,8},{41,9},{44,12},{45,13},{48,16},... | collective-permute-start | bytes 387080 | tf_op jit(solution)/shard_map/ppermute | solution.py:23
  32.8 3.6 %collective-permute-done.7 = bf16[24,2688]{1,0:T(8,128)(2,1)S(1)} collective-permute-done((bf16[24,2688]{1,0:T(8,128)(2,1)S(1)}, bf16[24,2688]{1,0:T(8,128)(2,1)S(1)}, u32[]{:S(2)}, u32[]{:S(2)}) %collective-permute-start.7) | collective-permute-done | bytes 129056 | tf_op jit(solution)/shard_map/ppermute | solution.py:23
  45.3 4.2 %collective-permute-done.10 = bf16[48,2688]{1,0:T(8,128)(2,1)S(1)} collective-permute-done((bf16[48,2688]{1,0:T(8,128)(2,1)S(1)}, bf16[48,2688]{1,0:T(8,128)(2,1)S(1)}, u32[]{:S(2)}, u32[]{:S(2)}) %collective-permute-start.10) | collective-permute-done | bytes 258080 | tf_op jit(solution)/shard_map/ppermute | solution.py:23
  49.5 3.4 %collective-permute-done.9 = bf16[48,2688]{1,0:T(8,128)(2,1)S(1)} collective-permute-done((bf16[48,2688]{1,0:T(8,128)(2,1)S(1)}, bf16[48,2688]{1,0:T(8,128)(2,1)S(1)}, u32[]{:S(2)}, u32[]{:S(2)}) %collective-permute-start.9) | collective-permute-done | bytes 258080 | tf_op jit(solution)/shard_map/ppermute | solution.py:23
  61.6 3.1 %collective-permute-start.16 = (bf16[72,2688]{1,0:T(8,128)(2,1)S(1)}, bf16[72,2688]{1,0:T(8,128)(2,1)S(1)}, u32[]{:S(2)}, u32[]{:S(2)}) collective-permute-start(bf16[72,2688]{1,0:T(8,128)(2,1)S(1)} %pad_maximum_fusion.8), channel_id=1, source_target_pairs={{32,0},{33,1},{36,4},{37,5},{40,8},{41,9},{44,12},{45,13},{48,16},... | collective-permute-start | bytes 1161224 | tf_op jit(solution)/shard_map/ppermute | solution.py:23
  64.7 3.2 %collective-permute-start.19 = (bf16[32,2688]{1,0:T(8,128)(2,1)S(1)}, bf16[32,2688]{1,0:T(8,128)(2,1)S(1)}, u32[]{:S(2)}, u32[]{:S(2)}) collective-permute-start(bf16[32,2688]{1,0:T(8,128)(2,1)S(1)} %pad_maximum_fusion.27), channel_id=1, source_target_pairs={{32,0},{33,1},{36,4},{37,5},{40,8},{41,9},{44,12},{45,13},{48,16},... | collective-permute-start | bytes 516104 | tf_op jit(solution)/shard_map/ppermute | solution.py:23
  68.1 6.5 %collective-permute-done.19 = bf16[32,2688]{1,0:T(8,128)(2,1)S(1)} collective-permute-done((bf16[32,2688]{1,0:T(8,128)(2,1)S(1)}, bf16[32,2688]{1,0:T(8,128)(2,1)S(1)}, u32[]{:S(2)}, u32[]{:S(2)}) %collective-permute-start.19) | collective-permute-done | bytes 172064 | tf_op jit(solution)/shard_map/ppermute | solution.py:23
  74.7 3.8 %collective-permute-start.20 = (bf16[72,2688]{1,0:T(8,128)(2,1)S(1)}, bf16[72,2688]{1,0:T(8,128)(2,1)S(1)}, u32[]{:S(2)}, u32[]{:S(2)}) collective-permute-start(bf16[72,2688]{1,0:T(8,128)(2,1)S(1)} %pad_maximum_fusion.10), channel_id=1, source_target_pairs={{32,0},{33,1},{36,4},{37,5},{40,8},{41,9},{44,12},{45,13},{48,16},... | collective-permute-start | bytes 1161224 | tf_op jit(solution)/shard_map/ppermute | solution.py:23
  79.0 4.7 %collective-permute-done.20 = bf16[72,2688]{1,0:T(8,128)(2,1)S(1)} collective-permute-done((bf16[72,2688]{1,0:T(8,128)(2,1)S(1)}, bf16[72,2688]{1,0:T(8,128)(2,1)S(1)}, u32[]{:S(2)}, u32[]{:S(2)}) %collective-permute-start.20) | collective-permute-done | bytes 387104 | tf_op jit(solution)/shard_map/ppermute | solution.py:23
  83.7 4.0 %collective-permute-done.18 = bf16[72,2688]{1,0:T(8,128)(2,1)S(1)} collective-permute-done((bf16[72,2688]{1,0:T(8,128)(2,1)S(1)}, bf16[72,2688]{1,0:T(8,128)(2,1)S(1)}, u32[]{:S(2)}, u32[]{:S(2)}) %collective-permute-start.18) | collective-permute-done | bytes 387104 | tf_op jit(solution)/shard_map/ppermute | solution.py:23
  88.2 3.2 %collective-permute-start.22 = (bf16[192,1792]{1,0:T(8,128)(2,1)S(1)}, bf16[192,1792]{1,0:T(8,128)(2,1)S(1)}, u32[]{:S(2)}, u32[]{:S(2)}) collective-permute-start(bf16[192,1792]{1,0:T(8,128)(2,1)S(1)} %pad_maximum_fusion.5), channel_id=1, source_target_pairs={{32,0},{33,1},{36,4},{37,5},{40,8},{41,9},{44,12},{45,13},{48,16},... | collective-permute-start | bytes 2064392 | tf_op jit(solution)/shard_map/ppermute | solution.py:23
  91.6 12.1 %collective-permute-done.21 = bf16[192,1792]{1,0:T(8,128)(2,1)S(1)} collective-permute-done((bf16[192,1792]{1,0:T(8,128)(2,1)S(1)}, bf16[192,1792]{1,0:T(8,128)(2,1)S(1)}, u32[]{:S(2)}, u32[]{:S(2)}) %collective-permute-start.21) | collective-permute-done | bytes 688160 | tf_op jit(solution)/shard_map/ppermute | solution.py:23
  103.8 3.3 %collective-permute-start.24 = (bf16[96,1792]{1,0:T(8,128)(2,1)S(1)}, bf16[96,1792]{1,0:T(8,128)(2,1)S(1)}, u32[]{:S(2)}, u32[]{:S(2)}) collective-permute-start(bf16[96,1792]{1,0:T(8,128)(2,1)S(1)} %slice.335), channel_id=1, source_target_pairs={{32,0},{33,1},{36,4},{37,5},{40,8},{41,9},{44,12},{45,13},{48,16},... | collective-permute-start | bytes 1032200 | tf_op jit(solution)/shard_map/ppermute | solution.py:23
  107.4 3.2 %collective-permute-start.26 = (bf16[192,896]{1,0:T(8,128)(2,1)S(1)}, bf16[192,896]{1,0:T(8,128)(2,1)S(1)}, u32[]{:S(2)}, u32[]{:S(2)}) collective-permute-start(bf16[192,896]{1,0:T(8,128)(2,1)S(1)} %fusion.21), channel_id=1, source_target_pairs={{32,0},{33,1},{36,4},{37,5},{40,8},{41,9},{44,12},{45,13},{48,16},... | collective-permute-start | bytes 1032200 | tf_op jit(solution)/shard_map/ppermute | solution.py:23
  113.9 3.0 %convolution_convert_fusion.3 = bf16[384,2048]{1,0:T(8,128)(2,1)S(1)} fusion(bf16[384,1792]{1,0:T(8,128)(2,1)S(1)} %bitcast.171, bf16[2048,1792]{1,0:T(8,128)(2,1)S(1)} %bitcast.129), kind=kOutput, calls=%fused_computation.5 | convolution fusion | flops 2819358720 | bytes 10289152 | tf_op jit(solution)/shard_map/dot_general | solution.py:43
  117.3 3.3 %collective-permute-start.32 = (bf16[96,896]{1,0:T(8,128)(2,1)S(1)}, bf16[96,896]{1,0:T(8,128)(2,1)S(1)}, u32[]{:S(2)}, u32[]{:S(2)}) collective-permute-start(bf16[96,896]{1,0:T(8,128)(2,1)S(1)} %slice.347), channel_id=1, source_target_pairs={{32,0},{33,1},{36,4},{37,5},{40,8},{41,9},{44,12},{45,13},{48,16},... | collective-permute-start | bytes 516104 | tf_op jit(solution)/shard_map/ppermute | solution.py:23
  120.6 3.0 %fusion.64 = f32[384,2048]{1,0:T(8,128)S(1)} fusion(bf16[384,1792]{1,0:T(8,128)(2,1)S(1)} %bitcast.170, bf16[2048,1792]{1,0:T(8,128)(2,1)S(1)} %bitcast.129), kind=kOutput, calls=%fused_computation.175 | convolution fusion | flops 2818572288 | bytes 11862016 | tf_op jit(solution)/shard_map/dot_general | solution.py:43
  132.4 4.9 %convolution_convert_fusion.1 = bf16[2048,896]{1,0:T(8,128)(2,1)} fusion(bf16[768,2048]{1,0:T(8,128)(2,1)S(1)} %constant_dynamic-update-slice_fusion.2, bf16[768,896]{1,0:T(8,128)(2,1)S(1)} %get-tuple-element.67), kind=kOutput, calls=%fused_computation.2 | convolution fusion | flops 2820407296 | bytes 8192000 | tf_op jit(solution)/shard_map/dot_general | solution.py:47
  137.4 5.0 %convolution_convert_fusion.2 = bf16[2048,896]{1,0:T(8,128)(2,1)} fusion(bf16[768,2048]{1,0:T(8,128)(2,1)S(1)} %constant_dynamic-update-slice_fusion.2, bf16[768,896]{1,0:T(8,128)(2,1)S(1)} %get-tuple-element.66), kind=kOutput, calls=%fused_computation.3 | convolution fusion | flops 2820407296 | bytes 8192000 | tf_op jit(solution)/shard_map/dot_general | solution.py:47
  147.0 4.5 %convolution_convert_fusion = bf16[896,2048]{1,0:T(8,128)(2,1)} fusion(bf16[768,896]{1,0:T(8,128)(2,1)S(1)} %bitcast.169, bf16[768,2048]{1,0:T(8,128)(2,1)S(1)} %constant_dynamic-update-slice_fusion.8), kind=kOutput, calls=%fused_computation.1 | convolution fusion | flops 2820407296 | bytes 8192000 | tf_op jit(solution)/shard_map/dot_general | solution.py:47
  (153 shorter events, 47.4 us)
Async XLA Ops:
  2.4 12.6 %collective-permute-start = (bf16[48,2048]{1,0:T(8,128)(2,1)S(1)}, bf16[48,2048]{1,0:T(8,128)(2,1)S(1)}, u32[]{:S(2)}, u32[]{:S(2)}) collective-permute-start(bf16[48,2048]{1,0:T(8,128)(2,1)S(1)} %constant_dynamic-update-slice_fusion), channel_id=1, source_target_pairs={{8,0},{3,1},{12,4},{7,5},{0,8},{11,9},{4,12},{15,13},{24,16},{19,1... | collective-permute-start | bytes 589832 | tf_op jit(solution)/shard_map/ppermute | solution.py:23
  15.3 21.1 %collective-permute-start.4 = (bf16[2,96,2048]{2,1,0:T(8,128)(2,1)S(1)}, bf16[2,96,2048]{2,1,0:T(8,128)(2,1)S(1)}, u32[]{:S(2)}, u32[]{:S(2)}) collective-permute-start(bf16[2,96,2048]{2,1,0:T(8,128)(2,1)S(1)} %bitcast.139), channel_id=1, source_target_pairs={{2,0},{9,1},{6,4},{13,5},{10,8},{1,9},{14,12},{5,13},{18,16},{25,1... | collective-permute-start | bytes 2359304 | tf_op jit(solution)/shard_map/ppermute | solution.py:23
  18.4 19.0 %collective-permute-start.5 = (bf16[2,96,2048]{2,1,0:T(8,128)(2,1)S(1)}, bf16[2,96,2048]{2,1,0:T(8,128)(2,1)S(1)}, u32[]{:S(2)}, u32[]{:S(2)}) collective-permute-start(bf16[2,96,2048]{2,1,0:T(8,128)(2,1)S(1)} %bitcast.140), channel_id=1, source_target_pairs={{16,0},{5,1},{20,4},{9,5},{24,8},{13,9},{28,12},{1,13},{2,16},{21,... | collective-permute-start | bytes 2359304 | tf_op jit(solution)/shard_map/ppermute | solution.py:23
  19.6 17.9 %collective-permute-start.6 = (bf16[2,96,2048]{2,1,0:T(8,128)(2,1)S(1)}, bf16[2,96,2048]{2,1,0:T(8,128)(2,1)S(1)}, u32[]{:S(2)}, u32[]{:S(2)}) collective-permute-start(bf16[2,96,2048]{2,1,0:T(8,128)(2,1)S(1)} %bitcast.141), channel_id=1, source_target_pairs={{18,0},{13,1},{22,4},{1,5},{26,8},{5,9},{30,12},{9,13},{0,16},{29,... | collective-permute-start | bytes 2359304 | tf_op jit(solution)/shard_map/ppermute | solution.py:23
  40.2 15.6 %collective-permute-start.12 = (bf16[288,2048]{1,0:T(8,128)(2,1)S(1)}, bf16[288,2048]{1,0:T(8,128)(2,1)S(1)}, u32[]{:S(2)}, u32[]{:S(2)}) collective-permute-start(bf16[288,2048]{1,0:T(8,128)(2,1)S(1)} %pad_maximum_fusion.4), channel_id=1, source_target_pairs={{1,0},{0,1},{5,4},{4,5},{9,8},{8,9},{13,12},{12,13},{17,16},{16,17... | collective-permute-start | bytes 3538952 | tf_op jit(solution)/shard_map/ppermute | solution.py:23
  40.3 15.5 %collective-permute-start.11 = (bf16[288,2048]{1,0:T(8,128)(2,1)S(1)}, bf16[288,2048]{1,0:T(8,128)(2,1)S(1)}, u32[]{:S(2)}, u32[]{:S(2)}) collective-permute-start(bf16[288,2048]{1,0:T(8,128)(2,1)S(1)} %pad_maximum_fusion.3), channel_id=1, source_target_pairs={{1,0},{0,1},{5,4},{4,5},{9,8},{8,9},{13,12},{12,13},{17,16},{16,17... | collective-permute-start | bytes 3538952 | tf_op jit(solution)/shard_map/ppermute | solution.py:23
  40.8 8.7 %collective-permute-start.10 = (bf16[48,2688]{1,0:T(8,128)(2,1)S(1)}, bf16[48,2688]{1,0:T(8,128)(2,1)S(1)}, u32[]{:S(2)}, u32[]{:S(2)}) collective-permute-start(bf16[48,2688]{1,0:T(8,128)(2,1)S(1)} %pad_maximum_fusion.25), channel_id=1, source_target_pairs={{32,0},{33,1},{36,4},{37,5},{40,8},{41,9},{44,12},{45,13},{48,16},... | collective-permute-start | bytes 774152 | tf_op jit(solution)/shard_map/ppermute | solution.py:23
  43.8 9.1 %collective-permute-start.9 = (bf16[48,2688]{1,0:T(8,128)(2,1)S(1)}, bf16[48,2688]{1,0:T(8,128)(2,1)S(1)}, u32[]{:S(2)}, u32[]{:S(2)}) collective-permute-start(bf16[48,2688]{1,0:T(8,128)(2,1)S(1)} %pad_maximum_fusion.24), channel_id=1, source_target_pairs={{96,0},{97,1},{100,4},{101,5},{104,8},{105,9},{108,12},{109,13},{1... | collective-permute-start | bytes 774152 | tf_op jit(solution)/shard_map/ppermute | solution.py:23
  61.2 17.3 %collective-permute-start.15 = (bf16[72,2688]{1,0:T(8,128)(2,1)S(1)}, bf16[72,2688]{1,0:T(8,128)(2,1)S(1)}, u32[]{:S(2)}, u32[]{:S(2)}) collective-permute-start(bf16[72,2688]{1,0:T(8,128)(2,1)S(1)} %pad_maximum_fusion.7), channel_id=1, source_target_pairs={{96,0},{97,1},{100,4},{101,5},{104,8},{105,9},{108,12},{109,13},{1... | collective-permute-start | bytes 1161224 | tf_op jit(solution)/shard_map/ppermute | solution.py:23
  61.6 17.0 %collective-permute-start.16 = (bf16[72,2688]{1,0:T(8,128)(2,1)S(1)}, bf16[72,2688]{1,0:T(8,128)(2,1)S(1)}, u32[]{:S(2)}, u32[]{:S(2)}) collective-permute-start(bf16[72,2688]{1,0:T(8,128)(2,1)S(1)} %pad_maximum_fusion.8), channel_id=1, source_target_pairs={{32,0},{33,1},{36,4},{37,5},{40,8},{41,9},{44,12},{45,13},{48,16},... | collective-permute-start | bytes 1161224 | tf_op jit(solution)/shard_map/ppermute | solution.py:23
  64.7 13.7 %collective-permute-start.17 = (bf16[40,2688]{1,0:T(8,128)(2,1)S(1)}, bf16[40,2688]{1,0:T(8,128)(2,1)S(1)}, u32[]{:S(2)}, u32[]{:S(2)}) collective-permute-start(bf16[40,2688]{1,0:T(8,128)(2,1)S(1)} %fusion.40), channel_id=1, source_target_pairs={{96,0},{97,1},{100,4},{101,5},{104,8},{105,9},{108,12},{109,13},{1... | collective-permute-start | bytes 645128 | tf_op jit(solution)/shard_map/ppermute | solution.py:23
  64.7 9.9 %collective-permute-start.19 = (bf16[32,2688]{1,0:T(8,128)(2,1)S(1)}, bf16[32,2688]{1,0:T(8,128)(2,1)S(1)}, u32[]{:S(2)}, u32[]{:S(2)}) collective-permute-start(bf16[32,2688]{1,0:T(8,128)(2,1)S(1)} %pad_maximum_fusion.27), channel_id=1, source_target_pairs={{32,0},{33,1},{36,4},{37,5},{40,8},{41,9},{44,12},{45,13},{48,16},... | collective-permute-start | bytes 516104 | tf_op jit(solution)/shard_map/ppermute | solution.py:23
  74.7 9.0 %collective-permute-start.20 = (bf16[72,2688]{1,0:T(8,128)(2,1)S(1)}, bf16[72,2688]{1,0:T(8,128)(2,1)S(1)}, u32[]{:S(2)}, u32[]{:S(2)}) collective-permute-start(bf16[72,2688]{1,0:T(8,128)(2,1)S(1)} %pad_maximum_fusion.10), channel_id=1, source_target_pairs={{32,0},{33,1},{36,4},{37,5},{40,8},{41,9},{44,12},{45,13},{48,16},... | collective-permute-start | bytes 1161224 | tf_op jit(solution)/shard_map/ppermute | solution.py:23
  78.5 9.2 %collective-permute-start.18 = (bf16[72,2688]{1,0:T(8,128)(2,1)S(1)}, bf16[72,2688]{1,0:T(8,128)(2,1)S(1)}, u32[]{:S(2)}, u32[]{:S(2)}) collective-permute-start(bf16[72,2688]{1,0:T(8,128)(2,1)S(1)} %pad_maximum_fusion.9), channel_id=1, source_target_pairs={{96,0},{97,1},{100,4},{101,5},{104,8},{105,9},{108,12},{109,13},{1... | collective-permute-start | bytes 1161224 | tf_op jit(solution)/shard_map/ppermute | solution.py:23
  88.1 15.6 %collective-permute-start.21 = (bf16[192,1792]{1,0:T(8,128)(2,1)S(1)}, bf16[192,1792]{1,0:T(8,128)(2,1)S(1)}, u32[]{:S(2)}, u32[]{:S(2)}) collective-permute-start(bf16[192,1792]{1,0:T(8,128)(2,1)S(1)} %pad_maximum_fusion.5), channel_id=1, source_target_pairs={{96,0},{97,1},{100,4},{101,5},{104,8},{105,9},{108,12},{109,13},{1... | collective-permute-start | bytes 2064392 | tf_op jit(solution)/shard_map/ppermute | solution.py:23
  88.2 15.5 %collective-permute-start.22 = (bf16[192,1792]{1,0:T(8,128)(2,1)S(1)}, bf16[192,1792]{1,0:T(8,128)(2,1)S(1)}, u32[]{:S(2)}, u32[]{:S(2)}) collective-permute-start(bf16[192,1792]{1,0:T(8,128)(2,1)S(1)} %pad_maximum_fusion.5), channel_id=1, source_target_pairs={{32,0},{33,1},{36,4},{37,5},{40,8},{41,9},{44,12},{45,13},{48,16},... | collective-permute-start | bytes 2064392 | tf_op jit(solution)/shard_map/ppermute | solution.py:23
  103.7 9.6 %collective-permute-start.23 = (bf16[96,1792]{1,0:T(8,128)(2,1)S(1)}, bf16[96,1792]{1,0:T(8,128)(2,1)S(1)}, u32[]{:S(2)}, u32[]{:S(2)}) collective-permute-start(bf16[96,1792]{1,0:T(8,128)(2,1)S(1)} %slice.334), channel_id=1, source_target_pairs={{96,0},{97,1},{100,4},{101,5},{104,8},{105,9},{108,12},{109,13},{1... | collective-permute-start | bytes 1032200 | tf_op jit(solution)/shard_map/ppermute | solution.py:23
  103.8 9.5 %collective-permute-start.24 = (bf16[96,1792]{1,0:T(8,128)(2,1)S(1)}, bf16[96,1792]{1,0:T(8,128)(2,1)S(1)}, u32[]{:S(2)}, u32[]{:S(2)}) collective-permute-start(bf16[96,1792]{1,0:T(8,128)(2,1)S(1)} %slice.335), channel_id=1, source_target_pairs={{32,0},{33,1},{36,4},{37,5},{40,8},{41,9},{44,12},{45,13},{48,16},... | collective-permute-start | bytes 1032200 | tf_op jit(solution)/shard_map/ppermute | solution.py:23
  107.3 9.9 %collective-permute-start.25 = (bf16[192,896]{1,0:T(8,128)(2,1)S(1)}, bf16[192,896]{1,0:T(8,128)(2,1)S(1)}, u32[]{:S(2)}, u32[]{:S(2)}) collective-permute-start(bf16[192,896]{1,0:T(8,128)(2,1)S(1)} %fusion.21), channel_id=1, source_target_pairs={{96,0},{97,1},{100,4},{101,5},{104,8},{105,9},{108,12},{109,13},{1... | collective-permute-start | bytes 1032200 | tf_op jit(solution)/shard_map/ppermute | solution.py:23
  107.4 9.8 %collective-permute-start.26 = (bf16[192,896]{1,0:T(8,128)(2,1)S(1)}, bf16[192,896]{1,0:T(8,128)(2,1)S(1)}, u32[]{:S(2)}, u32[]{:S(2)}) collective-permute-start(bf16[192,896]{1,0:T(8,128)(2,1)S(1)} %fusion.21), channel_id=1, source_target_pairs={{32,0},{33,1},{36,4},{37,5},{40,8},{41,9},{44,12},{45,13},{48,16},... | collective-permute-start | bytes 1032200 | tf_op jit(solution)/shard_map/ppermute | solution.py:23
  126.2 16.1 %collective-permute-start.28 = (bf16[96,2048]{1,0:T(8,128)(2,1)S(1)}, bf16[96,2048]{1,0:T(8,128)(2,1)S(1)}, u32[]{:S(2)}, u32[]{:S(2)}) collective-permute-start(bf16[96,2048]{1,0:T(8,128)(2,1)S(1)} %get-tuple-element.91), channel_id=1, source_target_pairs={{2,0},{9,1},{6,4},{13,5},{10,8},{1,9},{14,12},{5,13},{18,16},{25,1... | collective-permute-start | bytes 1179656 | tf_op jit(solution)/shard_map/ppermute | solution.py:23
  129.2 13.1 %collective-permute-start.29 = (bf16[96,2048]{1,0:T(8,128)(2,1)S(1)}, bf16[96,2048]{1,0:T(8,128)(2,1)S(1)}, u32[]{:S(2)}, u32[]{:S(2)}) collective-permute-start(bf16[96,2048]{1,0:T(8,128)(2,1)S(1)} %get-tuple-element.90), channel_id=1, source_target_pairs={{18,0},{13,1},{22,4},{1,5},{26,8},{5,9},{30,12},{9,13},{0,16},{29,... | collective-permute-start | bytes 1179656 | tf_op jit(solution)/shard_map/ppermute | solution.py:23
  129.8 12.5 %collective-permute-start.30 = (bf16[96,2048]{1,0:T(8,128)(2,1)S(1)}, bf16[96,2048]{1,0:T(8,128)(2,1)S(1)}, u32[]{:S(2)}, u32[]{:S(2)}) collective-permute-start(bf16[96,2048]{1,0:T(8,128)(2,1)S(1)} %get-tuple-element.89), channel_id=1, source_target_pairs={{16,0},{5,1},{20,4},{9,5},{24,8},{13,9},{28,12},{1,13},{2,16},{21,... | collective-permute-start | bytes 1179656 | tf_op jit(solution)/shard_map/ppermute | solution.py:23
  142.6 9.0 %collective-permute-start.33 = (f32[24,2048]{1,0:T(8,128)S(1)}, f32[24,2048]{1,0:T(8,128)S(1)}, u32[]{:S(2)}, u32[]{:S(2)}) collective-permute-start(f32[24,2048]{1,0:T(8,128)S(1)} %get-tuple-element.110), channel_id=1, source_target_pairs={{8,0},{3,1},{12,4},{7,5},{0,8},{11,9},{4,12},{15,13},{24,16},{19,1... | collective-permute-start | bytes 589832 | tf_op jit(solution)/shard_map/ppermute | solution.py:23
  (15 other events, 111.4 us)

commit v2 on v1

--- a/solution.py
+++ b/solution.py
@@ -1,6 +1,8 @@
 import jax
 import jax.numpy as jnp
 from jax import lax
+from jax.experimental import pallas as pl
+from jax.experimental.pallas import tpu as pltpu
 from jax.sharding import PartitionSpec as P
 
 ALL = ("depth", "row", "col")
@@ -104,6 +106,28 @@
 def spread_across(before, after):
     half = before.shape[0] // 2
     return cat(from_y(before[:half], -1), from_y(after[half:], 1))
+
+
+def weight_grads_kernel(tok_ref, delta_ref, gate_ref, up_ref):
+    both = inner(tok_ref[...], delta_ref[...])
+    half = gate_ref.shape[1]
+    gate_ref[...] = both[:, :half].astype(BF)
+    up_ref[...] = both[:, half:].astype(BF)
+
+
+def weight_grads(tok, delta):
+    (rows, width), both = tok.shape, delta.shape[1]
+    tile = min(width, 512)
+    out = jax.ShapeDtypeStruct((width, both // 2), BF)
+    return pl.pallas_call(
+        weight_grads_kernel,
+        grid=(width // tile,),
+        in_specs=[pl.BlockSpec((rows, tile), lambda i: (0, i)), pl.BlockSpec((rows, both), lambda i: (0, 0))],
+        out_specs=[pl.BlockSpec((tile, both // 2), lambda i: (i, 0))] * 2,
+        out_shape=[out, out],
+        cost_estimate=pl.CostEstimate(flops=2 * rows * width * both, bytes_accessed=4 * width * both, transcendentals=0),
+        compiler_params=pltpu.CompilerParams(vmem_limit_bytes=24 * 2**20),
+    )(tok, delta)
 
 
 def body(tokens, cotangent, gate_weight, up_weight, down_weight):
@@ -155,10 +179,9 @@
     part_other = other_core(outer(delta[384:], weights).astype(BF))
     part_own, part_other = together(outer(delta_own, weights), part_other)
     part = part_own + part_other.astype(F32)
-    part_bf, gate_delta, up_delta = together(part.astype(BF), delta[:, :896], delta[:, 896:])
+    part_bf, delta = together(part.astype(BF), delta)
     tok, cot = cat(tok_0[:96], tok_a, tok_0[96:], tok_b), cat(cot_0[:96], cot_a, cot_0[96:], cot_b)
-    gate_grad = inner(tok, gate_delta).astype(BF)
-    up_grad = inner(tok, up_delta).astype(BF)
+    gate_grad, up_grad = weight_grads(tok, delta)
     gate_grad, up_grad, *parts = together(
         gate_grad, up_grad, *[far(part_bf[96 * n : 96 * n + 96], -k) for n, k in ((3, 2), (1, 1), (2, 3))]
     )

time: 153 us -> 151 us (0.987)
  matrix products: 34.2 us -> 24.2 us
  Pallas kernels: 0 us -> 7.81 us
    dot_general x3 -> x1, matrix products: 14.4 us -> 4.52 us  [inner(): lax.dot_general(left, right, (((0,), (0,)), ((), ())), preferred_element_...]
    pallas_call x0 -> x1, Pallas kernels: none -> 7.81 us  [weight_grads(): pl.pallas_call(weight_grads_kernel, grid=(width // tile,), in_specs=[pl.B...]
  transfers between devices with their start and end apart: 36 -> 36, of which waited for: 13 -> 13; matrix products, arithmetic and copies ran while one was open for 27% -> 21% of each run, Pallas kernels for 0% -> 5%
where the time goes in v2:
time: 151 us
  starting transfers between devices  54.8 us (36%)
  waiting for transfers between devices  48.1 us (32%)
  matrix products  24.2 us (16%)
  other arithmetic  10.4 us (7%)
  Pallas kernels  7.81 us (5%)
  local copies, waits for them, and re-layouts  3.9 us (3%)
  between operations  1.56 us (1%)
    ppermute x36, starting transfers between devices, pull(): return lax.ppermute(a, ALL, pairs)  54.8 us
    ppermute x36, waiting for transfers between devices, pull(): return lax.ppermute(a, ALL, pairs)  48.1 us
    dot_general x5, matrix products, outer(): lax.dot_general(left, right, (((1,), (1,)), ((), ())), preferred_element_...  10.2 us
    dot_general x3, matrix products, dot(): return jnp.dot(left, right, preferred_element_type=F32)  9.49 us
    concatenate x23, other arithmetic, cat(): return jnp.concatenate(parts, axis=axis)  7.85 us
    pallas_call x1, Pallas kernels, weight_grads(): pl.pallas_call(weight_grads_kernel, grid=(width // tile,), in_specs=[pl.B...  7.81 us
    dot_general x1, matrix products, inner(): lax.dot_general(left, right, (((0,), (0,)), ((), ())), preferred_element_...  4.52 us
  transfers between devices with their start and end apart: 36, of which 13 were waited for; matrix products, arithmetic and copies ran while one was open for 21% of the time, Pallas kernels for 5%

profile of v2, /device:TPU:0, one launch (start us, length us, event | category | flops | bytes accessed | tf_op | source)
XLA Modules:
  0.0 150.8 jit_solution(10106763581569263834)
XLA Ops:
  2.4 4.0 %collective-permute-start = (bf16[48,2048]{1,0:T(8,128)(2,1)S(1)}, bf16[48,2048]{1,0:T(8,128)(2,1)S(1)}, u32[]{:S(2)}, u32[]{:S(2)}) collective-permute-start(bf16[48,2048]{1,0:T(8,128)(2,1)S(1)} %constant_dynamic-update-slice_fusion), channel_id=1, source_target_pairs={{8,0},{3,1},{12,4},{7,5},{0,8},{11,9},{4,12},{15,13},{24,16},{19,1... | collective-permute-start | bytes 589832 | tf_op jit(solution)/shard_map/ppermute | solution.py:25
  8.4 6.6 %pad_maximum_fusion = bf16[2048,1792]{1,0:T(8,128)(2,1)} fusion(bf16[2048,896]{1,0:T(8,128)(2,1)} %param.8, bf16[2048,896]{1,0:T(8,128)(2,1)} %param.7), kind=kLoop, calls=%fused_computation | loop fusion | flops 14680064 | bytes 14680064 | tf_op jit(solution)/shard_map/concatenate | solution.py:57
  15.3 3.1 %collective-permute-start.4 = (bf16[2,96,2048]{2,1,0:T(8,128)(2,1)S(1)}, bf16[2,96,2048]{2,1,0:T(8,128)(2,1)S(1)}, u32[]{:S(2)}, u32[]{:S(2)}) collective-permute-start(bf16[2,96,2048]{2,1,0:T(8,128)(2,1)S(1)} %bitcast.143), channel_id=1, source_target_pairs={{2,0},{9,1},{6,4},{13,5},{10,8},{1,9},{14,12},{5,13},{18,16},{25,1... | collective-permute-start | bytes 2359304 | tf_op jit(solution)/shard_map/ppermute | solution.py:25
  20.7 4.8 %fusion = f32[192,1792]{1,0:T(8,128)S(1)} fusion(bf16[2048,1792]{1,0:T(8,128)(2,1)} %pad_maximum_fusion, bf16[96,2048]{1,0:T(8,128)(2,1)S(1)} %get-tuple-element.119, bf16[96,2048]{1,0:T(8,128)(2,1)S(1)} %bitcast.170), kind=kOutput, calls=%fused_computation.9 | convolution fusion | flops 1410859008 | bytes 9502720 | tf_op jit(solution)/shard_map/dot_general | solution.py:53
  27.1 3.1 %collective-permute-start.8 = (bf16[24,2688]{1,0:T(8,128)(2,1)S(1)}, bf16[24,2688]{1,0:T(8,128)(2,1)S(1)}, u32[]{:S(2)}, u32[]{:S(2)}) collective-permute-start(bf16[24,2688]{1,0:T(8,128)(2,1)S(1)} %get-tuple-element.135), channel_id=1, source_target_pairs={{32,0},{33,1},{36,4},{37,5},{40,8},{41,9},{44,12},{45,13},{48,16},... | collective-permute-start | bytes 387080 | tf_op jit(solution)/shard_map/ppermute | solution.py:25
  32.8 3.6 %collective-permute-done.7 = bf16[24,2688]{1,0:T(8,128)(2,1)S(1)} collective-permute-done((bf16[24,2688]{1,0:T(8,128)(2,1)S(1)}, bf16[24,2688]{1,0:T(8,128)(2,1)S(1)}, u32[]{:S(2)}, u32[]{:S(2)}) %collective-permute-start.7) | collective-permute-done | bytes 129056 | tf_op jit(solution)/shard_map/ppermute | solution.py:25
  40.8 3.0 %collective-permute-start.10 = (bf16[48,2688]{1,0:T(8,128)(2,1)S(1)}, bf16[48,2688]{1,0:T(8,128)(2,1)S(1)}, u32[]{:S(2)}, u32[]{:S(2)}) collective-permute-start(bf16[48,2688]{1,0:T(8,128)(2,1)S(1)} %pad_maximum_fusion.25), channel_id=1, source_target_pairs={{32,0},{33,1},{36,4},{37,5},{40,8},{41,9},{44,12},{45,13},{48,16},... | collective-permute-start | bytes 774152 | tf_op jit(solution)/shard_map/ppermute | solution.py:25
  45.3 4.2 %collective-permute-done.10 = bf16[48,2688]{1,0:T(8,128)(2,1)S(1)} collective-permute-done((bf16[48,2688]{1,0:T(8,128)(2,1)S(1)}, bf16[48,2688]{1,0:T(8,128)(2,1)S(1)}, u32[]{:S(2)}, u32[]{:S(2)}) %collective-permute-start.10) | collective-permute-done | bytes 258080 | tf_op jit(solution)/shard_map/ppermute | solution.py:25
  49.6 3.4 %collective-permute-done.9 = bf16[48,2688]{1,0:T(8,128)(2,1)S(1)} collective-permute-done((bf16[48,2688]{1,0:T(8,128)(2,1)S(1)}, bf16[48,2688]{1,0:T(8,128)(2,1)S(1)}, u32[]{:S(2)}, u32[]{:S(2)}) %collective-permute-start.9) | collective-permute-done | bytes 258080 | tf_op jit(solution)/shard_map/ppermute | solution.py:25
  61.7 3.1 %collective-permute-start.16 = (bf16[72,2688]{1,0:T(8,128)(2,1)S(1)}, bf16[72,2688]{1,0:T(8,128)(2,1)S(1)}, u32[]{:S(2)}, u32[]{:S(2)}) collective-permute-start(bf16[72,2688]{1,0:T(8,128)(2,1)S(1)} %pad_maximum_fusion.8), channel_id=1, source_target_pairs={{32,0},{33,1},{36,4},{37,5},{40,8},{41,9},{44,12},{45,13},{48,16},... | collective-permute-start | bytes 1161224 | tf_op jit(solution)/shard_map/ppermute | solution.py:25
  64.8 3.2 %collective-permute-start.19 = (bf16[32,2688]{1,0:T(8,128)(2,1)S(1)}, bf16[32,2688]{1,0:T(8,128)(2,1)S(1)}, u32[]{:S(2)}, u32[]{:S(2)}) collective-permute-start(bf16[32,2688]{1,0:T(8,128)(2,1)S(1)} %pad_maximum_fusion.27), channel_id=1, source_target_pairs={{32,0},{33,1},{36,4},{37,5},{40,8},{41,9},{44,12},{45,13},{48,16},... | collective-permute-start | bytes 516104 | tf_op jit(solution)/shard_map/ppermute | solution.py:25
  68.1 6.5 %collective-permute-done.19 = bf16[32,2688]{1,0:T(8,128)(2,1)S(1)} collective-permute-done((bf16[32,2688]{1,0:T(8,128)(2,1)S(1)}, bf16[32,2688]{1,0:T(8,128)(2,1)S(1)}, u32[]{:S(2)}, u32[]{:S(2)}) %collective-permute-start.19) | collective-permute-done | bytes 172064 | tf_op jit(solution)/shard_map/ppermute | solution.py:25
  74.7 3.8 %collective-permute-start.20 = (bf16[72,2688]{1,0:T(8,128)(2,1)S(1)}, bf16[72,2688]{1,0:T(8,128)(2,1)S(1)}, u32[]{:S(2)}, u32[]{:S(2)}) collective-permute-start(bf16[72,2688]{1,0:T(8,128)(2,1)S(1)} %pad_maximum_fusion.10), channel_id=1, source_target_pairs={{32,0},{33,1},{36,4},{37,5},{40,8},{41,9},{44,12},{45,13},{48,16},... | collective-permute-start | bytes 1161224 | tf_op jit(solution)/shard_map/ppermute | solution.py:25
  79.0 4.7 %collective-permute-done.20 = bf16[72,2688]{1,0:T(8,128)(2,1)S(1)} collective-permute-done((bf16[72,2688]{1,0:T(8,128)(2,1)S(1)}, bf16[72,2688]{1,0:T(8,128)(2,1)S(1)}, u32[]{:S(2)}, u32[]{:S(2)}) %collective-permute-start.20) | collective-permute-done | bytes 387104 | tf_op jit(solution)/shard_map/ppermute | solution.py:25
  83.7 4.0 %collective-permute-done.18 = bf16[72,2688]{1,0:T(8,128)(2,1)S(1)} collective-permute-done((bf16[72,2688]{1,0:T(8,128)(2,1)S(1)}, bf16[72,2688]{1,0:T(8,128)(2,1)S(1)}, u32[]{:S(2)}, u32[]{:S(2)}) %collective-permute-start.18) | collective-permute-done | bytes 387104 | tf_op jit(solution)/shard_map/ppermute | solution.py:25
  88.3 3.2 %collective-permute-start.22 = (bf16[192,1792]{1,0:T(8,128)(2,1)S(1)}, bf16[192,1792]{1,0:T(8,128)(2,1)S(1)}, u32[]{:S(2)}, u32[]{:S(2)}) collective-permute-start(bf16[192,1792]{1,0:T(8,128)(2,1)S(1)} %pad_maximum_fusion.5), channel_id=1, source_target_pairs={{32,0},{33,1},{36,4},{37,5},{40,8},{41,9},{44,12},{45,13},{48,16},... | collective-permute-start | bytes 2064392 | tf_op jit(solution)/shard_map/ppermute | solution.py:25
  91.7 12.1 %collective-permute-done.21 = bf16[192,1792]{1,0:T(8,128)(2,1)S(1)} collective-permute-done((bf16[192,1792]{1,0:T(8,128)(2,1)S(1)}, bf16[192,1792]{1,0:T(8,128)(2,1)S(1)}, u32[]{:S(2)}, u32[]{:S(2)}) %collective-permute-start.21) | collective-permute-done | bytes 688160 | tf_op jit(solution)/shard_map/ppermute | solution.py:25
  103.9 3.3 %collective-permute-start.24 = (bf16[96,1792]{1,0:T(8,128)(2,1)S(1)}, bf16[96,1792]{1,0:T(8,128)(2,1)S(1)}, u32[]{:S(2)}, u32[]{:S(2)}) collective-permute-start(bf16[96,1792]{1,0:T(8,128)(2,1)S(1)} %slice.329), channel_id=1, source_target_pairs={{32,0},{33,1},{36,4},{37,5},{40,8},{41,9},{44,12},{45,13},{48,16},... | collective-permute-start | bytes 1032200 | tf_op jit(solution)/shard_map/ppermute | solution.py:25
  107.4 3.2 %collective-permute-start.26 = (bf16[192,896]{1,0:T(8,128)(2,1)S(1)}, bf16[192,896]{1,0:T(8,128)(2,1)S(1)}, u32[]{:S(2)}, u32[]{:S(2)}) collective-permute-start(bf16[192,896]{1,0:T(8,128)(2,1)S(1)} %fusion.21), channel_id=1, source_target_pairs={{32,0},{33,1},{36,4},{37,5},{40,8},{41,9},{44,12},{45,13},{48,16},... | collective-permute-start | bytes 1032200 | tf_op jit(solution)/shard_map/ppermute | solution.py:25
  114.0 3.0 %convolution_convert_fusion.1 = bf16[384,2048]{1,0:T(8,128)(2,1)S(1)} fusion(bf16[384,1792]{1,0:T(8,128)(2,1)S(1)} %bitcast.175, bf16[2048,1792]{1,0:T(8,128)(2,1)S(1)} %bitcast.133), kind=kOutput, calls=%fused_computation.3 | convolution fusion | flops 2819358720 | bytes 10289152 | tf_op jit(solution)/shard_map/dot_general | solution.py:45
  117.5 3.3 %collective-permute-start.32 = (bf16[96,896]{1,0:T(8,128)(2,1)S(1)}, bf16[96,896]{1,0:T(8,128)(2,1)S(1)}, u32[]{:S(2)}, u32[]{:S(2)}) collective-permute-start(bf16[96,896]{1,0:T(8,128)(2,1)S(1)} %slice.339), channel_id=1, source_target_pairs={{32,0},{33,1},{36,4},{37,5},{40,8},{41,9},{44,12},{45,13},{48,16},... | collective-permute-start | bytes 516104 | tf_op jit(solution)/shard_map/ppermute | solution.py:25
  120.8 3.0 %fusion.63 = f32[384,2048]{1,0:T(8,128)S(1)} fusion(bf16[384,1792]{1,0:T(8,128)(2,1)S(1)} %bitcast.174, bf16[2048,1792]{1,0:T(8,128)(2,1)S(1)} %bitcast.133), kind=kOutput, calls=%fused_computation.172 | convolution fusion | flops 2818572288 | bytes 11862016 | tf_op jit(solution)/shard_map/dot_general | solution.py:45
  132.7 7.8 %shard_map.84 = (bf16[2048,896]{1,0:T(8,128)(2,1)}, bf16[2048,896]{1,0:T(8,128)(2,1)}) custom-call(bf16[768,2048]{1,0:T(8,128)(2,1)S(1)} %constant_dynamic-update-slice_fusion.2.tok_ref, bf16[768,1792]{1,0:T(8,128)(2,1)S(1)} %bitcast.131), custom_call_target="tpu_custom_call" | custom-call | flops 5637144576 | bytes 14680064 | tf_op jit(solution)/shard_map/pallas_call | solution.py:122
  145.4 4.5 %convolution_convert_fusion = bf16[896,2048]{1,0:T(8,128)(2,1)} fusion(bf16[768,896]{1,0:T(8,128)(2,1)S(1)} %bitcast.173, bf16[768,2048]{1,0:T(8,128)(2,1)S(1)} %constant_dynamic-update-slice_fusion.8), kind=kOutput, calls=%fused_computation.1 | convolution fusion | flops 2820407296 | bytes 8192000 | tf_op jit(solution)/shard_map/dot_general | solution.py:49
  (155 shorter events, 44.5 us)
Async XLA Ops:
  2.4 12.6 %collective-permute-start = (bf16[48,2048]{1,0:T(8,128)(2,1)S(1)}, bf16[48,2048]{1,0:T(8,128)(2,1)S(1)}, u32[]{:S(2)}, u32[]{:S(2)}) collective-permute-start(bf16[48,2048]{1,0:T(8,128)(2,1)S(1)} %constant_dynamic-update-slice_fusion), channel_id=1, source_target_pairs={{8,0},{3,1},{12,4},{7,5},{0,8},{11,9},{4,12},{15,13},{24,16},{19,1... | collective-permute-start | bytes 589832 | tf_op jit(solution)/shard_map/ppermute | solution.py:25
  15.3 21.1 %collective-permute-start.4 = (bf16[2,96,2048]{2,1,0:T(8,128)(2,1)S(1)}, bf16[2,96,2048]{2,1,0:T(8,128)(2,1)S(1)}, u32[]{:S(2)}, u32[]{:S(2)}) collective-permute-start(bf16[2,96,2048]{2,1,0:T(8,128)(2,1)S(1)} %bitcast.143), channel_id=1, source_target_pairs={{2,0},{9,1},{6,4},{13,5},{10,8},{1,9},{14,12},{5,13},{18,16},{25,1... | collective-permute-start | bytes 2359304 | tf_op jit(solution)/shard_map/ppermute | solution.py:25
  18.5 19.0 %collective-permute-start.5 = (bf16[2,96,2048]{2,1,0:T(8,128)(2,1)S(1)}, bf16[2,96,2048]{2,1,0:T(8,128)(2,1)S(1)}, u32[]{:S(2)}, u32[]{:S(2)}) collective-permute-start(bf16[2,96,2048]{2,1,0:T(8,128)(2,1)S(1)} %bitcast.144), channel_id=1, source_target_pairs={{16,0},{5,1},{20,4},{9,5},{24,8},{13,9},{28,12},{1,13},{2,16},{21,... | collective-permute-start | bytes 2359304 | tf_op jit(solution)/shard_map/ppermute | solution.py:25
  19.6 17.9 %collective-permute-start.6 = (bf16[2,96,2048]{2,1,0:T(8,128)(2,1)S(1)}, bf16[2,96,2048]{2,1,0:T(8,128)(2,1)S(1)}, u32[]{:S(2)}, u32[]{:S(2)}) collective-permute-start(bf16[2,96,2048]{2,1,0:T(8,128)(2,1)S(1)} %bitcast.145), channel_id=1, source_target_pairs={{18,0},{13,1},{22,4},{1,5},{26,8},{5,9},{30,12},{9,13},{0,16},{29,... | collective-permute-start | bytes 2359304 | tf_op jit(solution)/shard_map/ppermute | solution.py:25
  40.2 15.6 %collective-permute-start.12 = (bf16[288,2048]{1,0:T(8,128)(2,1)S(1)}, bf16[288,2048]{1,0:T(8,128)(2,1)S(1)}, u32[]{:S(2)}, u32[]{:S(2)}) collective-permute-start(bf16[288,2048]{1,0:T(8,128)(2,1)S(1)} %pad_maximum_fusion.4), channel_id=1, source_target_pairs={{1,0},{0,1},{5,4},{4,5},{9,8},{8,9},{13,12},{12,13},{17,16},{16,17... | collective-permute-start | bytes 3538952 | tf_op jit(solution)/shard_map/ppermute | solution.py:25
  40.3 15.6 %collective-permute-start.11 = (bf16[288,2048]{1,0:T(8,128)(2,1)S(1)}, bf16[288,2048]{1,0:T(8,128)(2,1)S(1)}, u32[]{:S(2)}, u32[]{:S(2)}) collective-permute-start(bf16[288,2048]{1,0:T(8,128)(2,1)S(1)} %pad_maximum_fusion.3), channel_id=1, source_target_pairs={{1,0},{0,1},{5,4},{4,5},{9,8},{8,9},{13,12},{12,13},{17,16},{16,17... | collective-permute-start | bytes 3538952 | tf_op jit(solution)/shard_map/ppermute | solution.py:25
  40.8 8.7 %collective-permute-start.10 = (bf16[48,2688]{1,0:T(8,128)(2,1)S(1)}, bf16[48,2688]{1,0:T(8,128)(2,1)S(1)}, u32[]{:S(2)}, u32[]{:S(2)}) collective-permute-start(bf16[48,2688]{1,0:T(8,128)(2,1)S(1)} %pad_maximum_fusion.25), channel_id=1, source_target_pairs={{32,0},{33,1},{36,4},{37,5},{40,8},{41,9},{44,12},{45,13},{48,16},... | collective-permute-start | bytes 774152 | tf_op jit(solution)/shard_map/ppermute | solution.py:25
  43.9 9.1 %collective-permute-start.9 = (bf16[48,2688]{1,0:T(8,128)(2,1)S(1)}, bf16[48,2688]{1,0:T(8,128)(2,1)S(1)}, u32[]{:S(2)}, u32[]{:S(2)}) collective-permute-start(bf16[48,2688]{1,0:T(8,128)(2,1)S(1)} %pad_maximum_fusion.24), channel_id=1, source_target_pairs={{96,0},{97,1},{100,4},{101,5},{104,8},{105,9},{108,12},{109,13},{1... | collective-permute-start | bytes 774152 | tf_op jit(solution)/shard_map/ppermute | solution.py:25
  61.3 17.3 %collective-permute-start.15 = (bf16[72,2688]{1,0:T(8,128)(2,1)S(1)}, bf16[72,2688]{1,0:T(8,128)(2,1)S(1)}, u32[]{:S(2)}, u32[]{:S(2)}) collective-permute-start(bf16[72,2688]{1,0:T(8,128)(2,1)S(1)} %pad_maximum_fusion.7), channel_id=1, source_target_pairs={{96,0},{97,1},{100,4},{101,5},{104,8},{105,9},{108,12},{109,13},{1... | collective-permute-start | bytes 1161224 | tf_op jit(solution)/shard_map/ppermute | solution.py:25
  61.7 17.0 %collective-permute-start.16 = (bf16[72,2688]{1,0:T(8,128)(2,1)S(1)}, bf16[72,2688]{1,0:T(8,128)(2,1)S(1)}, u32[]{:S(2)}, u32[]{:S(2)}) collective-permute-start(bf16[72,2688]{1,0:T(8,128)(2,1)S(1)} %pad_maximum_fusion.8), channel_id=1, source_target_pairs={{32,0},{33,1},{36,4},{37,5},{40,8},{41,9},{44,12},{45,13},{48,16},... | collective-permute-start | bytes 1161224 | tf_op jit(solution)/shard_map/ppermute | solution.py:25
  64.8 13.7 %collective-permute-start.17 = (bf16[40,2688]{1,0:T(8,128)(2,1)S(1)}, bf16[40,2688]{1,0:T(8,128)(2,1)S(1)}, u32[]{:S(2)}, u32[]{:S(2)}) collective-permute-start(bf16[40,2688]{1,0:T(8,128)(2,1)S(1)} %fusion.40), channel_id=1, source_target_pairs={{96,0},{97,1},{100,4},{101,5},{104,8},{105,9},{108,12},{109,13},{1... | collective-permute-start | bytes 645128 | tf_op jit(solution)/shard_map/ppermute | solution.py:25
  64.8 9.9 %collective-permute-start.19 = (bf16[32,2688]{1,0:T(8,128)(2,1)S(1)}, bf16[32,2688]{1,0:T(8,128)(2,1)S(1)}, u32[]{:S(2)}, u32[]{:S(2)}) collective-permute-start(bf16[32,2688]{1,0:T(8,128)(2,1)S(1)} %pad_maximum_fusion.27), channel_id=1, source_target_pairs={{32,0},{33,1},{36,4},{37,5},{40,8},{41,9},{44,12},{45,13},{48,16},... | collective-permute-start | bytes 516104 | tf_op jit(solution)/shard_map/ppermute | solution.py:25
  74.7 9.0 %collective-permute-start.20 = (bf16[72,2688]{1,0:T(8,128)(2,1)S(1)}, bf16[72,2688]{1,0:T(8,128)(2,1)S(1)}, u32[]{:S(2)}, u32[]{:S(2)}) collective-permute-start(bf16[72,2688]{1,0:T(8,128)(2,1)S(1)} %pad_maximum_fusion.10), channel_id=1, source_target_pairs={{32,0},{33,1},{36,4},{37,5},{40,8},{41,9},{44,12},{45,13},{48,16},... | collective-permute-start | bytes 1161224 | tf_op jit(solution)/shard_map/ppermute | solution.py:25
  78.6 9.2 %collective-permute-start.18 = (bf16[72,2688]{1,0:T(8,128)(2,1)S(1)}, bf16[72,2688]{1,0:T(8,128)(2,1)S(1)}, u32[]{:S(2)}, u32[]{:S(2)}) collective-permute-start(bf16[72,2688]{1,0:T(8,128)(2,1)S(1)} %pad_maximum_fusion.9), channel_id=1, source_target_pairs={{96,0},{97,1},{100,4},{101,5},{104,8},{105,9},{108,12},{109,13},{1... | collective-permute-start | bytes 1161224 | tf_op jit(solution)/shard_map/ppermute | solution.py:25
  88.2 15.6 %collective-permute-start.21 = (bf16[192,1792]{1,0:T(8,128)(2,1)S(1)}, bf16[192,1792]{1,0:T(8,128)(2,1)S(1)}, u32[]{:S(2)}, u32[]{:S(2)}) collective-permute-start(bf16[192,1792]{1,0:T(8,128)(2,1)S(1)} %pad_maximum_fusion.5), channel_id=1, source_target_pairs={{96,0},{97,1},{100,4},{101,5},{104,8},{105,9},{108,12},{109,13},{1... | collective-permute-start | bytes 2064392 | tf_op jit(solution)/shard_map/ppermute | solution.py:25
  88.3 15.5 %collective-permute-start.22 = (bf16[192,1792]{1,0:T(8,128)(2,1)S(1)}, bf16[192,1792]{1,0:T(8,128)(2,1)S(1)}, u32[]{:S(2)}, u32[]{:S(2)}) collective-permute-start(bf16[192,1792]{1,0:T(8,128)(2,1)S(1)} %pad_maximum_fusion.5), channel_id=1, source_target_pairs={{32,0},{33,1},{36,4},{37,5},{40,8},{41,9},{44,12},{45,13},{48,16},... | collective-permute-start | bytes 2064392 | tf_op jit(solution)/shard_map/ppermute | solution.py:25
  103.8 9.6 %collective-permute-start.23 = (bf16[96,1792]{1,0:T(8,128)(2,1)S(1)}, bf16[96,1792]{1,0:T(8,128)(2,1)S(1)}, u32[]{:S(2)}, u32[]{:S(2)}) collective-permute-start(bf16[96,1792]{1,0:T(8,128)(2,1)S(1)} %slice.328), channel_id=1, source_target_pairs={{96,0},{97,1},{100,4},{101,5},{104,8},{105,9},{108,12},{109,13},{1... | collective-permute-start | bytes 1032200 | tf_op jit(solution)/shard_map/ppermute | solution.py:25
  103.9 9.5 %collective-permute-start.24 = (bf16[96,1792]{1,0:T(8,128)(2,1)S(1)}, bf16[96,1792]{1,0:T(8,128)(2,1)S(1)}, u32[]{:S(2)}, u32[]{:S(2)}) collective-permute-start(bf16[96,1792]{1,0:T(8,128)(2,1)S(1)} %slice.329), channel_id=1, source_target_pairs={{32,0},{33,1},{36,4},{37,5},{40,8},{41,9},{44,12},{45,13},{48,16},... | collective-permute-start | bytes 1032200 | tf_op jit(solution)/shard_map/ppermute | solution.py:25
  107.3 10.1 %collective-permute-start.25 = (bf16[192,896]{1,0:T(8,128)(2,1)S(1)}, bf16[192,896]{1,0:T(8,128)(2,1)S(1)}, u32[]{:S(2)}, u32[]{:S(2)}) collective-permute-start(bf16[192,896]{1,0:T(8,128)(2,1)S(1)} %fusion.21), channel_id=1, source_target_pairs={{96,0},{97,1},{100,4},{101,5},{104,8},{105,9},{108,12},{109,13},{1... | collective-permute-start | bytes 1032200 | tf_op jit(solution)/shard_map/ppermute | solution.py:25
  107.4 10.0 %collective-permute-start.26 = (bf16[192,896]{1,0:T(8,128)(2,1)S(1)}, bf16[192,896]{1,0:T(8,128)(2,1)S(1)}, u32[]{:S(2)}, u32[]{:S(2)}) collective-permute-start(bf16[192,896]{1,0:T(8,128)(2,1)S(1)} %fusion.21), channel_id=1, source_target_pairs={{32,0},{33,1},{36,4},{37,5},{40,8},{41,9},{44,12},{45,13},{48,16},... | collective-permute-start | bytes 1032200 | tf_op jit(solution)/shard_map/ppermute | solution.py:25
  126.5 14.0 %collective-permute-start.28 = (bf16[96,2048]{1,0:T(8,128)(2,1)S(1)}, bf16[96,2048]{1,0:T(8,128)(2,1)S(1)}, u32[]{:S(2)}, u32[]{:S(2)}) collective-permute-start(bf16[96,2048]{1,0:T(8,128)(2,1)S(1)} %get-tuple-element.91), channel_id=1, source_target_pairs={{2,0},{9,1},{6,4},{13,5},{10,8},{1,9},{14,12},{5,13},{18,16},{25,1... | collective-permute-start | bytes 1179656 | tf_op jit(solution)/shard_map/ppermute | solution.py:25
  129.4 11.1 %collective-permute-start.29 = (bf16[96,2048]{1,0:T(8,128)(2,1)S(1)}, bf16[96,2048]{1,0:T(8,128)(2,1)S(1)}, u32[]{:S(2)}, u32[]{:S(2)}) collective-permute-start(bf16[96,2048]{1,0:T(8,128)(2,1)S(1)} %get-tuple-element.90), channel_id=1, source_target_pairs={{18,0},{13,1},{22,4},{1,5},{26,8},{5,9},{30,12},{9,13},{0,16},{29,... | collective-permute-start | bytes 1179656 | tf_op jit(solution)/shard_map/ppermute | solution.py:25
  130.0 10.5 %collective-permute-start.30 = (bf16[96,2048]{1,0:T(8,128)(2,1)S(1)}, bf16[96,2048]{1,0:T(8,128)(2,1)S(1)}, u32[]{:S(2)}, u32[]{:S(2)}) collective-permute-start(bf16[96,2048]{1,0:T(8,128)(2,1)S(1)} %get-tuple-element.89), channel_id=1, source_target_pairs={{16,0},{5,1},{20,4},{9,5},{24,8},{13,9},{28,12},{1,13},{2,16},{21,... | collective-permute-start | bytes 1179656 | tf_op jit(solution)/shard_map/ppermute | solution.py:25
  140.7 9.1 %collective-permute-start.33 = (f32[24,2048]{1,0:T(8,128)S(1)}, f32[24,2048]{1,0:T(8,128)S(1)}, u32[]{:S(2)}, u32[]{:S(2)}) collective-permute-start(f32[24,2048]{1,0:T(8,128)S(1)} %get-tuple-element.110), channel_id=1, source_target_pairs={{8,0},{3,1},{12,4},{7,5},{0,8},{11,9},{4,12},{15,13},{24,16},{19,1... | collective-permute-start | bytes 589832 | tf_op jit(solution)/shard_map/ppermute | solution.py:25
  (17 other events, 121.1 us)

commit v3 on v2

--- a/solution.py
+++ b/solution.py
@@ -137,12 +137,15 @@
     def products(tok, cot):
         return [dot(tok, weights), outer(cot, down_weight)]
 
-    tc = cat(tokens, cotangent)
+    low = jnp.array(-jnp.inf, BF)
+    rows = tokens.shape[0]
+    tc = jnp.maximum(
+        lax.pad(tokens, low, ((0, rows, 0), (0, 0, 0))), lax.pad(cotangent, low, ((rows, 0, 0), (0, 0, 0)))
+    )
     weights = cat(gate_weight, up_weight, axis=1)
     near_2, near_1, near_3, weights = together(near(tc, 2), near(tc, 1), near(tc, 3), weights)
-    first = jnp.zeros((2, 4, 24, width), BF)
-    for k, b in ((2, near_2), (1, near_1), (3, near_3), (0, tc)):
-        first = lax.dynamic_update_slice_in_dim(first, b.reshape(2, 1, 24, width), lax.rem(k - y + 4, 4), 1)
+    chips = [b.reshape(2, 24, width) for b in (tc, near_1, near_2, near_3)]
+    first = jnp.stack([lax.select_n(y, *[chips[(n + k) % 4] for k in range(4)]) for n in range(4)], axis=1)
     q0 = first.reshape(2, 96, width)
     o0 = other_core(q0)
     q2, q1, q3 = far(q0, 2), far(q0, 1), far(q0, 3)

time: 151 us -> 150 us (level)
  local copies, waits for them, and re-layouts: 3.9 us -> 1.95 us
where the time goes in v3:
time: 150 us
  starting transfers between devices  54.9 us (37%)
  waiting for transfers between devices  48 us (32%)
  matrix products  24.2 us (16%)
  other arithmetic  11.7 us (8%)
  Pallas kernels  7.81 us (5%)
  local copies, waits for them, and re-layouts  1.95 us (1%)
  between operations  1.57 us (1%)
    ppermute x36, starting transfers between devices, pull(): return lax.ppermute(a, ALL, pairs)  54.9 us
    ppermute x36, waiting for transfers between devices, pull(): return lax.ppermute(a, ALL, pairs)  48 us
    dot_general x5, matrix products, outer(): lax.dot_general(left, right, (((1,), (1,)), ((), ())), preferred_element_...  10.2 us
    dot_general x3, matrix products, dot(): return jnp.dot(left, right, preferred_element_type=F32)  9.48 us
    concatenate x23, other arithmetic, cat(): return jnp.concatenate(parts, axis=axis)  7.86 us
    pallas_call x1, Pallas kernels, weight_grads(): pl.pallas_call(weight_grads_kernel, grid=(width // tile,), in_specs=[pl.B...  7.81 us
    dot_general x1, matrix products, inner(): lax.dot_general(left, right, (((0,), (0,)), ((), ())), preferred_element_...  4.52 us
  transfers between devices with their start and end apart: 36, of which 13 were waited for; matrix products, arithmetic and copies ran while one was open for 21% of the time, Pallas kernels for 5%

profile of v3, /device:TPU:0, one launch (start us, length us, event | category | flops | bytes accessed | tf_op | source)
XLA Modules:
  0.0 150.2 jit_solution(7534588415080979201)
XLA Ops:
  1.6 4.0 %collective-permute-start = (bf16[48,2048]{1,0:T(8,128)(2,1)S(1)}, bf16[48,2048]{1,0:T(8,128)(2,1)S(1)}, u32[]{:S(2)}, u32[]{:S(2)}) collective-permute-start(bf16[48,2048]{1,0:T(8,128)(2,1)S(1)} %pad_maximum_fusion.28), channel_id=1, source_target_pairs={{8,0},{3,1},{12,4},{7,5},{0,8},{11,9},{4,12},{15,13},{24,16},{19,1... | collective-permute-start | bytes 589832 | tf_op jit(solution)/shard_map/ppermute | solution.py:25
  7.7 6.6 %pad_maximum_fusion = bf16[2048,1792]{1,0:T(8,128)(2,1)} fusion(bf16[2048,896]{1,0:T(8,128)(2,1)} %param.8, bf16[2048,896]{1,0:T(8,128)(2,1)} %param.7), kind=kLoop, calls=%fused_computation | loop fusion | flops 14680064 | bytes 14680064 | tf_op jit(solution)/shard_map/concatenate | solution.py:57
  14.8 3.1 %collective-permute-start.4 = (bf16[2,96,2048]{2,1,0:T(8,128)(2,1)S(1)}, bf16[2,96,2048]{2,1,0:T(8,128)(2,1)S(1)}, u32[]{:S(2)}, u32[]{:S(2)}) collective-permute-start(bf16[2,96,2048]{2,1,0:T(8,128)(2,1)S(1)} %bitcast.143), channel_id=1, source_target_pairs={{2,0},{9,1},{6,4},{13,5},{10,8},{1,9},{14,12},{5,13},{18,16},{25,1... | collective-permute-start | bytes 2359304 | tf_op jit(solution)/shard_map/ppermute | solution.py:25
  20.2 4.8 %fusion = f32[192,1792]{1,0:T(8,128)S(1)} fusion(bf16[2048,1792]{1,0:T(8,128)(2,1)} %pad_maximum_fusion, bf16[96,2048]{1,0:T(8,128)(2,1)S(1)} %get-tuple-element.119, bf16[96,2048]{1,0:T(8,128)(2,1)S(1)} %bitcast.170), kind=kOutput, calls=%fused_computation.10 | convolution fusion | flops 1410859008 | bytes 9502720 | tf_op jit(solution)/shard_map/dot_general | solution.py:53
  26.6 3.1 %collective-permute-start.8 = (bf16[24,2688]{1,0:T(8,128)(2,1)S(1)}, bf16[24,2688]{1,0:T(8,128)(2,1)S(1)}, u32[]{:S(2)}, u32[]{:S(2)}) collective-permute-start(bf16[24,2688]{1,0:T(8,128)(2,1)S(1)} %get-tuple-element.139), channel_id=1, source_target_pairs={{32,0},{33,1},{36,4},{37,5},{40,8},{41,9},{44,12},{45,13},{48,16},... | collective-permute-start | bytes 387080 | tf_op jit(solution)/shard_map/ppermute | solution.py:25
  32.2 3.6 %collective-permute-done.7 = bf16[24,2688]{1,0:T(8,128)(2,1)S(1)} collective-permute-done((bf16[24,2688]{1,0:T(8,128)(2,1)S(1)}, bf16[24,2688]{1,0:T(8,128)(2,1)S(1)}, u32[]{:S(2)}, u32[]{:S(2)}) %collective-permute-start.7) | collective-permute-done | bytes 129056 | tf_op jit(solution)/shard_map/ppermute | solution.py:25
  40.3 3.0 %collective-permute-start.10 = (bf16[48,2688]{1,0:T(8,128)(2,1)S(1)}, bf16[48,2688]{1,0:T(8,128)(2,1)S(1)}, u32[]{:S(2)}, u32[]{:S(2)}) collective-permute-start(bf16[48,2688]{1,0:T(8,128)(2,1)S(1)} %pad_maximum_fusion.26), channel_id=1, source_target_pairs={{32,0},{33,1},{36,4},{37,5},{40,8},{41,9},{44,12},{45,13},{48,16},... | collective-permute-start | bytes 774152 | tf_op jit(solution)/shard_map/ppermute | solution.py:25
  44.8 4.2 %collective-permute-done.10 = bf16[48,2688]{1,0:T(8,128)(2,1)S(1)} collective-permute-done((bf16[48,2688]{1,0:T(8,128)(2,1)S(1)}, bf16[48,2688]{1,0:T(8,128)(2,1)S(1)}, u32[]{:S(2)}, u32[]{:S(2)}) %collective-permute-start.10) | collective-permute-done | bytes 258080 | tf_op jit(solution)/shard_map/ppermute | solution.py:25
  49.0 3.4 %collective-permute-done.9 = bf16[48,2688]{1,0:T(8,128)(2,1)S(1)} collective-permute-done((bf16[48,2688]{1,0:T(8,128)(2,1)S(1)}, bf16[48,2688]{1,0:T(8,128)(2,1)S(1)}, u32[]{:S(2)}, u32[]{:S(2)}) %collective-permute-start.9) | collective-permute-done | bytes 258080 | tf_op jit(solution)/shard_map/ppermute | solution.py:25
  61.1 3.1 %collective-permute-start.16 = (bf16[72,2688]{1,0:T(8,128)(2,1)S(1)}, bf16[72,2688]{1,0:T(8,128)(2,1)S(1)}, u32[]{:S(2)}, u32[]{:S(2)}) collective-permute-start(bf16[72,2688]{1,0:T(8,128)(2,1)S(1)} %pad_maximum_fusion.9), channel_id=1, source_target_pairs={{32,0},{33,1},{36,4},{37,5},{40,8},{41,9},{44,12},{45,13},{48,16},... | collective-permute-start | bytes 1161224 | tf_op jit(solution)/shard_map/ppermute | solution.py:25
  64.2 3.2 %collective-permute-start.19 = (bf16[32,2688]{1,0:T(8,128)(2,1)S(1)}, bf16[32,2688]{1,0:T(8,128)(2,1)S(1)}, u32[]{:S(2)}, u32[]{:S(2)}) collective-permute-start(bf16[32,2688]{1,0:T(8,128)(2,1)S(1)} %pad_maximum_fusion.29), channel_id=1, source_target_pairs={{32,0},{33,1},{36,4},{37,5},{40,8},{41,9},{44,12},{45,13},{48,16},... | collective-permute-start | bytes 516104 | tf_op jit(solution)/shard_map/ppermute | solution.py:25
  67.6 6.5 %collective-permute-done.19 = bf16[32,2688]{1,0:T(8,128)(2,1)S(1)} collective-permute-done((bf16[32,2688]{1,0:T(8,128)(2,1)S(1)}, bf16[32,2688]{1,0:T(8,128)(2,1)S(1)}, u32[]{:S(2)}, u32[]{:S(2)}) %collective-permute-start.19) | collective-permute-done | bytes 172064 | tf_op jit(solution)/shard_map/ppermute | solution.py:25
  74.2 3.8 %collective-permute-start.20 = (bf16[72,2688]{1,0:T(8,128)(2,1)S(1)}, bf16[72,2688]{1,0:T(8,128)(2,1)S(1)}, u32[]{:S(2)}, u32[]{:S(2)}) collective-permute-start(bf16[72,2688]{1,0:T(8,128)(2,1)S(1)} %pad_maximum_fusion.11), channel_id=1, source_target_pairs={{32,0},{33,1},{36,4},{37,5},{40,8},{41,9},{44,12},{45,13},{48,16},... | collective-permute-start | bytes 1161224 | tf_op jit(solution)/shard_map/ppermute | solution.py:25
  78.5 4.7 %collective-permute-done.20 = bf16[72,2688]{1,0:T(8,128)(2,1)S(1)} collective-permute-done((bf16[72,2688]{1,0:T(8,128)(2,1)S(1)}, bf16[72,2688]{1,0:T(8,128)(2,1)S(1)}, u32[]{:S(2)}, u32[]{:S(2)}) %collective-permute-start.20) | collective-permute-done | bytes 387104 | tf_op jit(solution)/shard_map/ppermute | solution.py:25
  83.2 4.0 %collective-permute-done.18 = bf16[72,2688]{1,0:T(8,128)(2,1)S(1)} collective-permute-done((bf16[72,2688]{1,0:T(8,128)(2,1)S(1)}, bf16[72,2688]{1,0:T(8,128)(2,1)S(1)}, u32[]{:S(2)}, u32[]{:S(2)}) %collective-permute-start.18) | collective-permute-done | bytes 387104 | tf_op jit(solution)/shard_map/ppermute | solution.py:25
  87.7 3.2 %collective-permute-start.22 = (bf16[192,1792]{1,0:T(8,128)(2,1)S(1)}, bf16[192,1792]{1,0:T(8,128)(2,1)S(1)}, u32[]{:S(2)}, u32[]{:S(2)}) collective-permute-start(bf16[192,1792]{1,0:T(8,128)(2,1)S(1)} %pad_maximum_fusion.6), channel_id=1, source_target_pairs={{32,0},{33,1},{36,4},{37,5},{40,8},{41,9},{44,12},{45,13},{48,16},... | collective-permute-start | bytes 2064392 | tf_op jit(solution)/shard_map/ppermute | solution.py:25
  91.1 12.1 %collective-permute-done.21 = bf16[192,1792]{1,0:T(8,128)(2,1)S(1)} collective-permute-done((bf16[192,1792]{1,0:T(8,128)(2,1)S(1)}, bf16[192,1792]{1,0:T(8,128)(2,1)S(1)}, u32[]{:S(2)}, u32[]{:S(2)}) %collective-permute-start.21) | collective-permute-done | bytes 688160 | tf_op jit(solution)/shard_map/ppermute | solution.py:25
  103.3 3.3 %collective-permute-start.24 = (bf16[96,1792]{1,0:T(8,128)(2,1)S(1)}, bf16[96,1792]{1,0:T(8,128)(2,1)S(1)}, u32[]{:S(2)}, u32[]{:S(2)}) collective-permute-start(bf16[96,1792]{1,0:T(8,128)(2,1)S(1)} %slice.329), channel_id=1, source_target_pairs={{32,0},{33,1},{36,4},{37,5},{40,8},{41,9},{44,12},{45,13},{48,16},... | collective-permute-start | bytes 1032200 | tf_op jit(solution)/shard_map/ppermute | solution.py:25
  106.8 3.2 %collective-permute-start.26 = (bf16[192,896]{1,0:T(8,128)(2,1)S(1)}, bf16[192,896]{1,0:T(8,128)(2,1)S(1)}, u32[]{:S(2)}, u32[]{:S(2)}) collective-permute-start(bf16[192,896]{1,0:T(8,128)(2,1)S(1)} %fusion.21), channel_id=1, source_target_pairs={{32,0},{33,1},{36,4},{37,5},{40,8},{41,9},{44,12},{45,13},{48,16},... | collective-permute-start | bytes 1032200 | tf_op jit(solution)/shard_map/ppermute | solution.py:25
  113.5 3.0 %convolution_convert_fusion.1 = bf16[384,2048]{1,0:T(8,128)(2,1)S(1)} fusion(bf16[384,1792]{1,0:T(8,128)(2,1)S(1)} %bitcast.175, bf16[2048,1792]{1,0:T(8,128)(2,1)S(1)} %bitcast.133), kind=kOutput, calls=%fused_computation.3 | convolution fusion | flops 2819358720 | bytes 10289152 | tf_op jit(solution)/shard_map/dot_general | solution.py:45
  117.0 3.3 %collective-permute-start.32 = (bf16[96,896]{1,0:T(8,128)(2,1)S(1)}, bf16[96,896]{1,0:T(8,128)(2,1)S(1)}, u32[]{:S(2)}, u32[]{:S(2)}) collective-permute-start(bf16[96,896]{1,0:T(8,128)(2,1)S(1)} %slice.339), channel_id=1, source_target_pairs={{32,0},{33,1},{36,4},{37,5},{40,8},{41,9},{44,12},{45,13},{48,16},... | collective-permute-start | bytes 516104 | tf_op jit(solution)/shard_map/ppermute | solution.py:25
  120.3 3.0 %fusion.63 = f32[384,2048]{1,0:T(8,128)S(1)} fusion(bf16[384,1792]{1,0:T(8,128)(2,1)S(1)} %bitcast.174, bf16[2048,1792]{1,0:T(8,128)(2,1)S(1)} %bitcast.133), kind=kOutput, calls=%fused_computation.172 | convolution fusion | flops 2818572288 | bytes 11862016 | tf_op jit(solution)/shard_map/dot_general | solution.py:45
  132.1 7.8 %shard_map.84 = (bf16[2048,896]{1,0:T(8,128)(2,1)}, bf16[2048,896]{1,0:T(8,128)(2,1)}) custom-call(bf16[768,2048]{1,0:T(8,128)(2,1)S(1)} %constant_dynamic-update-slice_fusion.tok_ref, bf16[768,1792]{1,0:T(8,128)(2,1)S(1)} %bitcast.131), custom_call_target="tpu_custom_call" | custom-call | flops 5637144576 | bytes 14680064 | tf_op jit(solution)/shard_map/pallas_call | solution.py:122
  144.8 4.5 %convolution_convert_fusion = bf16[896,2048]{1,0:T(8,128)(2,1)} fusion(bf16[768,896]{1,0:T(8,128)(2,1)S(1)} %bitcast.173, bf16[768,2048]{1,0:T(8,128)(2,1)S(1)} %constant_dynamic-update-slice_fusion.6), kind=kOutput, calls=%fused_computation.1 | convolution fusion | flops 2820407296 | bytes 8192000 | tf_op jit(solution)/shard_map/dot_general | solution.py:49
  (155 shorter events, 43.9 us)
Async XLA Ops:
  1.6 12.7 %collective-permute-start = (bf16[48,2048]{1,0:T(8,128)(2,1)S(1)}, bf16[48,2048]{1,0:T(8,128)(2,1)S(1)}, u32[]{:S(2)}, u32[]{:S(2)}) collective-permute-start(bf16[48,2048]{1,0:T(8,128)(2,1)S(1)} %pad_maximum_fusion.28), channel_id=1, source_target_pairs={{8,0},{3,1},{12,4},{7,5},{0,8},{11,9},{4,12},{15,13},{24,16},{19,1... | collective-permute-start | bytes 589832 | tf_op jit(solution)/shard_map/ppermute | solution.py:25
  14.8 21.1 %collective-permute-start.4 = (bf16[2,96,2048]{2,1,0:T(8,128)(2,1)S(1)}, bf16[2,96,2048]{2,1,0:T(8,128)(2,1)S(1)}, u32[]{:S(2)}, u32[]{:S(2)}) collective-permute-start(bf16[2,96,2048]{2,1,0:T(8,128)(2,1)S(1)} %bitcast.143), channel_id=1, source_target_pairs={{2,0},{9,1},{6,4},{13,5},{10,8},{1,9},{14,12},{5,13},{18,16},{25,1... | collective-permute-start | bytes 2359304 | tf_op jit(solution)/shard_map/ppermute | solution.py:25
  17.9 19.0 %collective-permute-start.5 = (bf16[2,96,2048]{2,1,0:T(8,128)(2,1)S(1)}, bf16[2,96,2048]{2,1,0:T(8,128)(2,1)S(1)}, u32[]{:S(2)}, u32[]{:S(2)}) collective-permute-start(bf16[2,96,2048]{2,1,0:T(8,128)(2,1)S(1)} %bitcast.144), channel_id=1, source_target_pairs={{16,0},{5,1},{20,4},{9,5},{24,8},{13,9},{28,12},{1,13},{2,16},{21,... | collective-permute-start | bytes 2359304 | tf_op jit(solution)/shard_map/ppermute | solution.py:25
  19.0 17.9 %collective-permute-start.6 = (bf16[2,96,2048]{2,1,0:T(8,128)(2,1)S(1)}, bf16[2,96,2048]{2,1,0:T(8,128)(2,1)S(1)}, u32[]{:S(2)}, u32[]{:S(2)}) collective-permute-start(bf16[2,96,2048]{2,1,0:T(8,128)(2,1)S(1)} %bitcast.145), channel_id=1, source_target_pairs={{18,0},{13,1},{22,4},{1,5},{26,8},{5,9},{30,12},{9,13},{0,16},{29,... | collective-permute-start | bytes 2359304 | tf_op jit(solution)/shard_map/ppermute | solution.py:25
  39.7 15.6 %collective-permute-start.12 = (bf16[288,2048]{1,0:T(8,128)(2,1)S(1)}, bf16[288,2048]{1,0:T(8,128)(2,1)S(1)}, u32[]{:S(2)}, u32[]{:S(2)}) collective-permute-start(bf16[288,2048]{1,0:T(8,128)(2,1)S(1)} %pad_maximum_fusion.4), channel_id=1, source_target_pairs={{1,0},{0,1},{5,4},{4,5},{9,8},{8,9},{13,12},{12,13},{17,16},{16,17... | collective-permute-start | bytes 3538952 | tf_op jit(solution)/shard_map/ppermute | solution.py:25
  39.8 15.6 %collective-permute-start.11 = (bf16[288,2048]{1,0:T(8,128)(2,1)S(1)}, bf16[288,2048]{1,0:T(8,128)(2,1)S(1)}, u32[]{:S(2)}, u32[]{:S(2)}) collective-permute-start(bf16[288,2048]{1,0:T(8,128)(2,1)S(1)} %pad_maximum_fusion.3), channel_id=1, source_target_pairs={{1,0},{0,1},{5,4},{4,5},{9,8},{8,9},{13,12},{12,13},{17,16},{16,17... | collective-permute-start | bytes 3538952 | tf_op jit(solution)/shard_map/ppermute | solution.py:25
  40.3 8.8 %collective-permute-start.10 = (bf16[48,2688]{1,0:T(8,128)(2,1)S(1)}, bf16[48,2688]{1,0:T(8,128)(2,1)S(1)}, u32[]{:S(2)}, u32[]{:S(2)}) collective-permute-start(bf16[48,2688]{1,0:T(8,128)(2,1)S(1)} %pad_maximum_fusion.26), channel_id=1, source_target_pairs={{32,0},{33,1},{36,4},{37,5},{40,8},{41,9},{44,12},{45,13},{48,16},... | collective-permute-start | bytes 774152 | tf_op jit(solution)/shard_map/ppermute | solution.py:25
  43.3 9.1 %collective-permute-start.9 = (bf16[48,2688]{1,0:T(8,128)(2,1)S(1)}, bf16[48,2688]{1,0:T(8,128)(2,1)S(1)}, u32[]{:S(2)}, u32[]{:S(2)}) collective-permute-start(bf16[48,2688]{1,0:T(8,128)(2,1)S(1)} %pad_maximum_fusion.25), channel_id=1, source_target_pairs={{96,0},{97,1},{100,4},{101,5},{104,8},{105,9},{108,12},{109,13},{1... | collective-permute-start | bytes 774152 | tf_op jit(solution)/shard_map/ppermute | solution.py:25
  60.8 17.3 %collective-permute-start.15 = (bf16[72,2688]{1,0:T(8,128)(2,1)S(1)}, bf16[72,2688]{1,0:T(8,128)(2,1)S(1)}, u32[]{:S(2)}, u32[]{:S(2)}) collective-permute-start(bf16[72,2688]{1,0:T(8,128)(2,1)S(1)} %pad_maximum_fusion.8), channel_id=1, source_target_pairs={{96,0},{97,1},{100,4},{101,5},{104,8},{105,9},{108,12},{109,13},{1... | collective-permute-start | bytes 1161224 | tf_op jit(solution)/shard_map/ppermute | solution.py:25
  61.1 17.0 %collective-permute-start.16 = (bf16[72,2688]{1,0:T(8,128)(2,1)S(1)}, bf16[72,2688]{1,0:T(8,128)(2,1)S(1)}, u32[]{:S(2)}, u32[]{:S(2)}) collective-permute-start(bf16[72,2688]{1,0:T(8,128)(2,1)S(1)} %pad_maximum_fusion.9), channel_id=1, source_target_pairs={{32,0},{33,1},{36,4},{37,5},{40,8},{41,9},{44,12},{45,13},{48,16},... | collective-permute-start | bytes 1161224 | tf_op jit(solution)/shard_map/ppermute | solution.py:25
  64.2 13.7 %collective-permute-start.17 = (bf16[40,2688]{1,0:T(8,128)(2,1)S(1)}, bf16[40,2688]{1,0:T(8,128)(2,1)S(1)}, u32[]{:S(2)}, u32[]{:S(2)}) collective-permute-start(bf16[40,2688]{1,0:T(8,128)(2,1)S(1)} %fusion.40), channel_id=1, source_target_pairs={{96,0},{97,1},{100,4},{101,5},{104,8},{105,9},{108,12},{109,13},{1... | collective-permute-start | bytes 645128 | tf_op jit(solution)/shard_map/ppermute | solution.py:25
  64.2 9.9 %collective-permute-start.19 = (bf16[32,2688]{1,0:T(8,128)(2,1)S(1)}, bf16[32,2688]{1,0:T(8,128)(2,1)S(1)}, u32[]{:S(2)}, u32[]{:S(2)}) collective-permute-start(bf16[32,2688]{1,0:T(8,128)(2,1)S(1)} %pad_maximum_fusion.29), channel_id=1, source_target_pairs={{32,0},{33,1},{36,4},{37,5},{40,8},{41,9},{44,12},{45,13},{48,16},... | collective-permute-start | bytes 516104 | tf_op jit(solution)/shard_map/ppermute | solution.py:25
  74.2 9.0 %collective-permute-start.20 = (bf16[72,2688]{1,0:T(8,128)(2,1)S(1)}, bf16[72,2688]{1,0:T(8,128)(2,1)S(1)}, u32[]{:S(2)}, u32[]{:S(2)}) collective-permute-start(bf16[72,2688]{1,0:T(8,128)(2,1)S(1)} %pad_maximum_fusion.11), channel_id=1, source_target_pairs={{32,0},{33,1},{36,4},{37,5},{40,8},{41,9},{44,12},{45,13},{48,16},... | collective-permute-start | bytes 1161224 | tf_op jit(solution)/shard_map/ppermute | solution.py:25
  78.0 9.2 %collective-permute-start.18 = (bf16[72,2688]{1,0:T(8,128)(2,1)S(1)}, bf16[72,2688]{1,0:T(8,128)(2,1)S(1)}, u32[]{:S(2)}, u32[]{:S(2)}) collective-permute-start(bf16[72,2688]{1,0:T(8,128)(2,1)S(1)} %pad_maximum_fusion.10), channel_id=1, source_target_pairs={{96,0},{97,1},{100,4},{101,5},{104,8},{105,9},{108,12},{109,13},{1... | collective-permute-start | bytes 1161224 | tf_op jit(solution)/shard_map/ppermute | solution.py:25
  87.6 15.6 %collective-permute-start.21 = (bf16[192,1792]{1,0:T(8,128)(2,1)S(1)}, bf16[192,1792]{1,0:T(8,128)(2,1)S(1)}, u32[]{:S(2)}, u32[]{:S(2)}) collective-permute-start(bf16[192,1792]{1,0:T(8,128)(2,1)S(1)} %pad_maximum_fusion.6), channel_id=1, source_target_pairs={{96,0},{97,1},{100,4},{101,5},{104,8},{105,9},{108,12},{109,13},{1... | collective-permute-start | bytes 2064392 | tf_op jit(solution)/shard_map/ppermute | solution.py:25
  87.7 15.5 %collective-permute-start.22 = (bf16[192,1792]{1,0:T(8,128)(2,1)S(1)}, bf16[192,1792]{1,0:T(8,128)(2,1)S(1)}, u32[]{:S(2)}, u32[]{:S(2)}) collective-permute-start(bf16[192,1792]{1,0:T(8,128)(2,1)S(1)} %pad_maximum_fusion.6), channel_id=1, source_target_pairs={{32,0},{33,1},{36,4},{37,5},{40,8},{41,9},{44,12},{45,13},{48,16},... | collective-permute-start | bytes 2064392 | tf_op jit(solution)/shard_map/ppermute | solution.py:25
  103.2 9.6 %collective-permute-start.23 = (bf16[96,1792]{1,0:T(8,128)(2,1)S(1)}, bf16[96,1792]{1,0:T(8,128)(2,1)S(1)}, u32[]{:S(2)}, u32[]{:S(2)}) collective-permute-start(bf16[96,1792]{1,0:T(8,128)(2,1)S(1)} %slice.328), channel_id=1, source_target_pairs={{96,0},{97,1},{100,4},{101,5},{104,8},{105,9},{108,12},{109,13},{1... | collective-permute-start | bytes 1032200 | tf_op jit(solution)/shard_map/ppermute | solution.py:25
  103.3 9.5 %collective-permute-start.24 = (bf16[96,1792]{1,0:T(8,128)(2,1)S(1)}, bf16[96,1792]{1,0:T(8,128)(2,1)S(1)}, u32[]{:S(2)}, u32[]{:S(2)}) collective-permute-start(bf16[96,1792]{1,0:T(8,128)(2,1)S(1)} %slice.329), channel_id=1, source_target_pairs={{32,0},{33,1},{36,4},{37,5},{40,8},{41,9},{44,12},{45,13},{48,16},... | collective-permute-start | bytes 1032200 | tf_op jit(solution)/shard_map/ppermute | solution.py:25
  106.7 10.1 %collective-permute-start.25 = (bf16[192,896]{1,0:T(8,128)(2,1)S(1)}, bf16[192,896]{1,0:T(8,128)(2,1)S(1)}, u32[]{:S(2)}, u32[]{:S(2)}) collective-permute-start(bf16[192,896]{1,0:T(8,128)(2,1)S(1)} %fusion.21), channel_id=1, source_target_pairs={{96,0},{97,1},{100,4},{101,5},{104,8},{105,9},{108,12},{109,13},{1... | collective-permute-start | bytes 1032200 | tf_op jit(solution)/shard_map/ppermute | solution.py:25
  106.8 10.0 %collective-permute-start.26 = (bf16[192,896]{1,0:T(8,128)(2,1)S(1)}, bf16[192,896]{1,0:T(8,128)(2,1)S(1)}, u32[]{:S(2)}, u32[]{:S(2)}) collective-permute-start(bf16[192,896]{1,0:T(8,128)(2,1)S(1)} %fusion.21), channel_id=1, source_target_pairs={{32,0},{33,1},{36,4},{37,5},{40,8},{41,9},{44,12},{45,13},{48,16},... | collective-permute-start | bytes 1032200 | tf_op jit(solution)/shard_map/ppermute | solution.py:25
  125.9 14.0 %collective-permute-start.28 = (bf16[96,2048]{1,0:T(8,128)(2,1)S(1)}, bf16[96,2048]{1,0:T(8,128)(2,1)S(1)}, u32[]{:S(2)}, u32[]{:S(2)}) collective-permute-start(bf16[96,2048]{1,0:T(8,128)(2,1)S(1)} %get-tuple-element.91), channel_id=1, source_target_pairs={{2,0},{9,1},{6,4},{13,5},{10,8},{1,9},{14,12},{5,13},{18,16},{25,1... | collective-permute-start | bytes 1179656 | tf_op jit(solution)/shard_map/ppermute | solution.py:25
  128.9 11.1 %collective-permute-start.29 = (bf16[96,2048]{1,0:T(8,128)(2,1)S(1)}, bf16[96,2048]{1,0:T(8,128)(2,1)S(1)}, u32[]{:S(2)}, u32[]{:S(2)}) collective-permute-start(bf16[96,2048]{1,0:T(8,128)(2,1)S(1)} %get-tuple-element.90), channel_id=1, source_target_pairs={{18,0},{13,1},{22,4},{1,5},{26,8},{5,9},{30,12},{9,13},{0,16},{29,... | collective-permute-start | bytes 1179656 | tf_op jit(solution)/shard_map/ppermute | solution.py:25
  129.5 10.5 %collective-permute-start.30 = (bf16[96,2048]{1,0:T(8,128)(2,1)S(1)}, bf16[96,2048]{1,0:T(8,128)(2,1)S(1)}, u32[]{:S(2)}, u32[]{:S(2)}) collective-permute-start(bf16[96,2048]{1,0:T(8,128)(2,1)S(1)} %get-tuple-element.89), channel_id=1, source_target_pairs={{16,0},{5,1},{20,4},{9,5},{24,8},{13,9},{28,12},{1,13},{2,16},{21,... | collective-permute-start | bytes 1179656 | tf_op jit(solution)/shard_map/ppermute | solution.py:25
  140.2 9.2 %collective-permute-start.33 = (f32[24,2048]{1,0:T(8,128)S(1)}, f32[24,2048]{1,0:T(8,128)S(1)}, u32[]{:S(2)}, u32[]{:S(2)}) collective-permute-start(f32[24,2048]{1,0:T(8,128)S(1)} %get-tuple-element.110), channel_id=1, source_target_pairs={{8,0},{3,1},{12,4},{7,5},{0,8},{11,9},{4,12},{15,13},{24,16},{19,1... | collective-permute-start | bytes 589832 | tf_op jit(solution)/shard_map/ppermute | solution.py:25
  (19 other events, 146.5 us)
